TPU v7x, 256 devices: a whole 4x4x8 slice. The times are simulated.
256 devices in a mesh: space: 64 (over z, x, core), inst: 4 (over y).
Axes of the slice: x: 4, y: 4, z: 8, core: 2. Of those that a mesh axis runs over, the one named last changes fastest.
Arguments:
- start: float32 [16, 7, 131072], P('inst', None, 'space'), may hold values from -14 to 14
- shifted_diag: float32 [131072], P('space'), may hold values from -1 to 1
- face_coef: float32 [6, 131072], P(None, 'space'), may hold values from 0.03 to 0.15
- mixing: float32 [7, 7], replicated, may hold values from -2 to 2
- neighbours: int32 [6, 131072], P(None, 'space'), may hold values from 0 to 2559, as said below
- basis: float32 [20, 16, 7, 131072], P(None, 'inst', None, 'space'), may hold values from -13 to 13
Outputs:
- block: float32 [4, 16, 7, 131072], P(None, 'inst', None, 'space')
- proj: float32 [20, 4], replicated
- factor: float32 [4, 4], replicated
Inputs may be any that keep to these rules, and one draw needn't show every extreme that they name: `neighbours`: faces 0 and 1 of a cell name the cell one layer below and above it; faces 2 to 5 name cells of the same layer.
All inputs are finite; a program needn't handle non-finite values.
Results may differ from a plain program's by a relative error of at most 0.00026.
Values sent between devices are 32-bit elements; how exact they have to be, the bound alone decides.
A program may use at most 64 MiB of HBM per device.

v0:
```python
import math

import jax
import jax.numpy as jnp
from jax import lax
from jax.sharding import PartitionSpec as P

NT = 16
VARS = 7
S = 4
FACES = 6
FACE = 256


def padded(array, sides, width):
    for axis, dim in sides:
        peers, length = (lax.axis_size(axis), array.shape[dim])
        up = [(i, (i + 1) % peers) for i in range(peers - 1)]
        down = [(j, i) for i, j in up]
        last = lax.slice_in_dim(array, length - width, length, axis=dim)
        initial = lax.slice_in_dim(array, 0, width, axis=dim)
        before = lax.ppermute(last, axis, up)
        after = lax.ppermute(initial, axis, down)
        array = jnp.concatenate([before, array, after], axis=dim)
    return array


def spectral_rows(rows, cols):
    idiff = rows[:, None] - cols[None, :]
    angle = idiff.astype(jnp.float32) * jnp.float32(math.pi / NT)
    parity = jnp.where(idiff % 2 == 0, jnp.float32(1.0), jnp.float32(-1.0))
    safe = jnp.where(idiff == 0, jnp.float32(1.0), jnp.sin(angle))
    return jnp.where(idiff == 0, jnp.float32(0.0), 0.5 * parity * jnp.cos(angle) / safe)


def operate(middle, source, face_index, diagonal, coefficients, mixing, derive):
    count = middle.shape[2]
    layer_count = count // FACE
    below_vals = source[:, :, :count]
    above_vals = source[:, :, 2 * FACE : 2 * FACE + count]
    within_pos = (face_index[2:] % FACE).reshape(FACES - 2, layer_count, FACE)
    onehot = (
        within_pos[:, :, :, None] == jnp.arange(FACE, dtype=jnp.int32)[None, None, None, :]
    ).astype(jnp.float32)
    layered = middle.reshape(middle.shape[0], middle.shape[1], layer_count, FACE)
    within_vals = jnp.einsum("flts,njls->fnjlt", onehot, layered, precision=lax.Precision.HIGHEST)
    within_vals = within_vals.reshape(FACES - 2, middle.shape[0], middle.shape[1], count)
    flux = coefficients[0] * (middle - below_vals)
    flux = flux + coefficients[1] * (middle - above_vals)
    for face in range(2, FACES):
        flux = flux + coefficients[face] * (middle - within_vals[face - 2])
    mixed = jnp.einsum("ij,njc->nic", mixing, flux, precision=lax.Precision.HIGHEST)
    timed = 0.1 * derive(middle)
    return diagonal * middle + timed + mixed


def shards(start, shifted_diag, face_coef, mixing, neighbours, basis):
    local_steps = start.shape[0]
    cell_dev = start.shape[2]
    first = lax.axis_index("inst") * local_steps
    mine = first + jnp.arange(local_steps, dtype=jnp.int32)
    every = jnp.arange(NT, dtype=jnp.int32)
    current = start
    my_rows = spectral_rows(mine, every)

    def derive(field):
        return jnp.einsum(
            "nk,kjc->njc",
            my_rows,
            lax.all_gather(field, "inst", axis=0, tiled=True),
            precision=lax.Precision.HIGHEST,
        )

    vectors = []
    for step in range(S):
        source = padded(current, (("space", 2),), FACE)
        current = operate(current, source, neighbours, shifted_diag, face_coef, mixing, derive)
        vectors.append(current)
    krylov = jnp.stack(vectors)
    total_count = jnp.float32(NT * VARS * cell_dev * lax.axis_size("space"))
    proj_part = jnp.einsum("bnjc,snjc->bs", basis, krylov, precision=lax.Precision.HIGHEST)
    proj = lax.psum(proj_part, ("space", "inst")) / total_count
    projected = krylov - jnp.einsum("bs,bnjc->snjc", proj, basis, precision=lax.Precision.HIGHEST)
    gram_part = jnp.einsum("snjc,tnjc->st", projected, projected, precision=lax.Precision.HIGHEST)
    gram = lax.psum(gram_part, ("space", "inst")) / total_count
    lower = jnp.linalg.cholesky(gram)
    inverse = jax.scipy.linalg.solve_triangular(lower, jnp.eye(S, dtype=jnp.float32), lower=True)
    block = jnp.einsum("st,tnjc->snjc", inverse, projected, precision=lax.Precision.HIGHEST)
    return (block, proj, lower.T)


def solution(mesh):
    return jax.shard_map(
        shards,
        mesh=mesh,
        in_specs=(
            P("inst", None, "space"),
            P("space"),
            P(None, "space"),
            P(),
            P(None, "space"),
            P(None, "inst", None, "space"),
        ),
        out_specs=(P(None, "inst", None, "space"), P(), P()),
        check_vma=False,
    )
```

profile of v0, /device:TPU:1, one launch (start us, length us, event | category | flops | bytes accessed | tf_op | source)
XLA Modules:
  0.0 319.5 jit_solution(15128570976819428308)
XLA Ops:
  0.6 0.8 fusion.158
  1.4 4.5 %collective-permute-start = (f32[4,7,256]{2,0,1:T(4,128)S(1)}, f32[4,7,256]{2,0,1:T(4,128)S(1)}, u32[]{:S(2)}, u32[]{:S(2)}) collective-permute-start(f32[4,7,256]{2,0,1:T(4,128)S(1)} %get-tuple-element.31), channel_id=1, source_target_pairs={{0,4},{4,8},{8,12},{12,16},{16,20},{20,24},{24,28},{28,32},{32,36}... | collective-permute-start | bytes 86024 | tf_op jit(solution)/shard_map/ppermute | solution.py:22
  5.9 1.9 collective-permute-start.1
  7.9 1.1 reshape.76
  8.9 1.1 copy.50
  10.0 1.1 fusion.159
  11.1 0.9 add_select_fusion
  12.0 5.5 %fusion.27 = f32[4,4,7,8,256]{4,2,1,0,3:T(8,128)S(1)} fusion(s32[4,8,256]{2,0,1:T(4,128)S(1)} %bitcast.205, f32[4,7,8,256,1]{3,2,0,1,4:T(8,128)S(1)} %bitcast.177), kind=kOutput, calls=%fused_computation.28 | convolution fusion | flops 706740224 | bytes 1179648 | tf_op jit(solution)/shard_map/flts,njls->fnjlt/dot_general | solution.py:46
  17.7 14.4 %all_gather.12 = f32[16,7,2048]{2,1,0:T(8,128)S(1)} all-gather(f32[4,7,2048]{2,1,0:T(8,128)S(1)} %copy.50), channel_id=1, replica_groups=mesh['space'=64,'inst'=4] {'inst'}, dimensions={0}, use_global_device_ids=true | all-gather | bytes 1146880 | tf_op jit(solution)/shard_map/all_gather | solution.py:70
  33.2 0.3 fusion.95
  33.5 0.5 fusion.60
  34.0 1.3 fusion.19
  35.6 5.9 %fusion.30 = f32[4,4,7,8,256]{4,2,0,1,3:T(8,128)S(1)} fusion(s32[4,8,256]{2,0,1:T(4,128)S(1)} %bitcast.206, f32[4,7,8,256,1]{3,2,0,1,4:T(8,128)S(1)} %bitcast.179), kind=kOutput, calls=%fused_computation.29 | convolution fusion | flops 706740224 | bytes 1179648 | tf_op jit(solution)/shard_map/flts,njls->fnjlt/dot_general | solution.py:46
  41.5 4.5 %collective-permute-start.2 = (f32[4,7,256]{2,0,1:T(4,128)S(1)}, f32[4,7,256]{2,0,1:T(4,128)S(1)}, u32[]{:S(2)}, u32[]{:S(2)}) collective-permute-start(f32[4,7,256]{2,0,1:T(4,128)S(1)} %get-tuple-element.29), channel_id=1, source_target_pairs={{0,4},{4,8},{8,12},{12,16},{16,20},{20,24},{24,28},{28,32},{32,36}... | collective-permute-start | bytes 86024 | tf_op jit(solution)/shard_map/ppermute | solution.py:22
  46.0 1.9 collective-permute-start.3
  47.9 13.2 %all_gather.13 = f32[16,7,2048]{2,1,0:T(8,128)S(1)} all-gather(f32[4,7,2048]{2,1,0:T(8,128)S(1)} %copy.60), channel_id=1, replica_groups=mesh['space'=64,'inst'=4] {'inst'}, dimensions={0}, use_global_device_ids=true | all-gather | bytes 1146880 | tf_op jit(solution)/shard_map/all_gather | solution.py:70
  62.4 0.3 fusion.86
  62.7 0.5 fusion.58
  63.2 1.3 fusion.21
  64.7 5.9 %fusion.33 = f32[4,4,7,8,256]{4,2,0,1,3:T(8,128)S(1)} fusion(s32[4,8,256]{2,0,1:T(4,128)S(1)} %bitcast.207, f32[4,7,8,256,1]{3,2,0,1,4:T(8,128)S(1)} %bitcast.180), kind=kOutput, calls=%fused_computation.30 | convolution fusion | flops 706740224 | bytes 1179648 | tf_op jit(solution)/shard_map/flts,njls->fnjlt/dot_general | solution.py:46
  70.6 5.7 %collective-permute-start.4 = (f32[4,7,256]{2,0,1:T(4,128)S(1)}, f32[4,7,256]{2,0,1:T(4,128)S(1)}, u32[]{:S(2)}, u32[]{:S(2)}) collective-permute-start(f32[4,7,256]{2,0,1:T(4,128)S(1)} %get-tuple-element.27), channel_id=1, source_target_pairs={{0,4},{4,8},{8,12},{12,16},{16,20},{20,24},{24,28},{28,32},{32,36}... | collective-permute-start | bytes 86024 | tf_op jit(solution)/shard_map/ppermute | solution.py:22
  76.3 1.9 collective-permute-start.5
  78.2 12.4 %all_gather.14 = f32[16,7,2048]{2,1,0:T(8,128)S(1)} all-gather(f32[4,7,2048]{2,1,0:T(8,128)S(1)} %copy.69), channel_id=1, replica_groups=mesh['space'=64,'inst'=4] {'inst'}, dimensions={0}, use_global_device_ids=true | all-gather | bytes 1146880 | tf_op jit(solution)/shard_map/all_gather | solution.py:70
  91.8 0.3 fusion.77
  92.1 0.5 fusion.56
  92.6 1.3 fusion.23
  94.1 5.9 %fusion.36 = f32[4,4,7,8,256]{4,2,0,1,3:T(8,128)S(1)} fusion(s32[4,8,256]{2,0,1:T(4,128)S(1)} %bitcast.208, f32[4,7,8,256,1]{3,2,0,1,4:T(8,128)S(1)} %bitcast.178), kind=kOutput, calls=%fused_computation.31 | convolution fusion | flops 706740224 | bytes 1179648 | tf_op jit(solution)/shard_map/flts,njls->fnjlt/dot_general | solution.py:46
  100.0 6.9 %collective-permute-start.6 = (f32[4,7,256]{2,0,1:T(4,128)S(1)}, f32[4,7,256]{2,0,1:T(4,128)S(1)}, u32[]{:S(2)}, u32[]{:S(2)}) collective-permute-start(f32[4,7,256]{2,0,1:T(4,128)S(1)} %get-tuple-element.25), channel_id=1, source_target_pairs={{0,4},{4,8},{8,12},{12,16},{16,20},{20,24},{24,28},{28,32},{32,36}... | collective-permute-start | bytes 86024 | tf_op jit(solution)/shard_map/ppermute | solution.py:22
  106.9 1.9 collective-permute-start.7
  108.8 13.7 %all_gather.15 = f32[16,7,2048]{2,1,0:T(8,128)S(1)} all-gather(f32[4,7,2048]{2,1,0:T(8,128)S(1)} %copy.78), channel_id=1, replica_groups=mesh['space'=64,'inst'=4] {'inst'}, dimensions={0}, use_global_device_ids=true | all-gather | bytes 1146880 | tf_op jit(solution)/shard_map/all_gather | solution.py:70
  123.7 0.3 fusion.68
  124.0 0.5 fusion.54
  124.5 1.3 fusion.26
  125.8 0.2 pad_maximum_fusion
  126.0 9.6 %fusion.39 = f32[20,4]{0,1:T(4,128)S(1)} fusion(f32[20,4,7,2048]{3,1,2,0:T(4,128)} %param.11, f32[4,4,7,2048]{3,1,2,0:T(4,128)S(1)} %pad_maximum_fusion), kind=kOutput, calls=%fused_computation.32 | convolution fusion | flops 55050240 | bytes 5505344 | tf_op jit(solution)/shard_map/bnjc,snjc->bs/dot_general | solution.py:81
  135.6 89.7 %psum.14 = f32[20,4]{0,1:T(4,128)S(1)} all-reduce(f32[20,4]{0,1:T(4,128)S(1)} %fusion.39), channel_id=1, replica_groups=mesh['space'=64,'inst'=4] {'space','inst'}, use_global_device_ids=true, to_apply=%region_0.1 | all-reduce | flops 80 | bytes 640 | tf_op jit(solution)/shard_map/psum | solution.py:82
  225.4 7.6 %fusion.10 = f32[4,4,7,2048]{3,0,2,1:T(4,128)S(1)} fusion(f32[20,4,7,2048]{3,1,2,0:T(4,128)} %param.11, f32[20,4]{0,1:T(4,128)S(1)} %broadcast_multiply_fusion.1), kind=kOutput, calls=%fused_computation.7 | convolution fusion | flops 55050240 | bytes 5505344 | tf_op jit(solution)/shard_map/bs,bnjc->snjc/dot_general | solution.py:83
  233.0 0.8 copy_subtract_fusion
  233.8 4.1 %convolution_bitcast_fusion.1 = f32[4,4]{0,1:T(4,128)S(1)} fusion(f32[4,4,7,2048]{3,1,2,0:T(4,128)S(1)} %copy_subtract_fusion), kind=kOutput, calls=%fused_computation.34 | convolution fusion | flops 11010048 | bytes 917568 | tf_op jit(solution)/shard_map/snjc,tnjc->st/dot_general | solution.py:84
  237.9 75.0 %psum.15 = f32[4,4]{0,1:T(4,128)S(1)} all-reduce(f32[4,4]{0,1:T(4,128)S(1)} %convolution_bitcast_fusion.1), channel_id=1, replica_groups=mesh['space'=64,'inst'=4] {'space','inst'}, use_global_device_ids=true, to_apply=%region_1.2 | all-reduce | flops 16 | bytes 128 | tf_op jit(solution)/shard_map/psum | solution.py:85
  313.0 0.4 cholesky.17
  313.4 0.6 compare_reduce_fusion
  314.0 0.6 fusion.114
  314.7 0.3 custom-call.7
  315.0 0.2 convolution_bitcast_fusion
  315.2 2.1 fusion.42
  317.3 1.5 copy.97
  318.8 0.7 copy.98
  (67 shorter events, 5.4 us)
Async XLA Ops:
  0.6 32.9 %copy-start = (f32[7,7]{1,0:T(8,128)S(1)}, f32[7,7]{1,0:T(8,128)}, u32[]{:S(2)}) copy-start(f32[7,7]{1,0:T(8,128)} %param.9) | copy-start | bytes 592
  1.4 31.7 %collective-permute-start = (f32[4,7,256]{2,0,1:T(4,128)S(1)}, f32[4,7,256]{2,0,1:T(4,128)S(1)}, u32[]{:S(2)}, u32[]{:S(2)}) collective-permute-start(f32[4,7,256]{2,0,1:T(4,128)S(1)} %get-tuple-element.31), channel_id=1, source_target_pairs={{0,4},{4,8},{8,12},{12,16},{16,20},{20,24},{24,28},{28,32},{32,36}... | collective-permute-start | bytes 86024 | tf_op jit(solution)/shard_map/ppermute | solution.py:22
  5.9 27.3 %collective-permute-start.1 = (f32[4,7,256]{2,0,1:T(4,128)S(1)}, f32[4,7,256]{2,0,1:T(4,128)S(1)}, u32[]{:S(2)}, u32[]{:S(2)}) collective-permute-start(f32[4,7,256]{2,0,1:T(4,128)S(1)} %get-tuple-element.32), channel_id=1, source_target_pairs={{4,0},{8,4},{12,8},{16,12},{20,16},{24,20},{28,24},{32,28},{36,32}... | collective-permute-start | bytes 86024 | tf_op jit(solution)/shard_map/ppermute | solution.py:23
  17.6 15.6 %copy-start.1 = (f32[4,7,2048]{2,0,1:T(4,128)S(1)}, f32[4,7,2048]{2,0,1:T(4,128)}, u32[]{:S(2)}) copy-start(f32[4,7,2048]{2,0,1:T(4,128)} %param.6) | copy-start | bytes 688132
  17.6 16.4 %copy-start.2 = (f32[2048]{0:T(1024)S(1)}, f32[2048]{0:T(1024)}, u32[]{:S(2)}) copy-start(f32[2048]{0:T(1024)} %param.7) | copy-start | bytes 24580
  41.5 20.9 %collective-permute-start.2 = (f32[4,7,256]{2,0,1:T(4,128)S(1)}, f32[4,7,256]{2,0,1:T(4,128)S(1)}, u32[]{:S(2)}, u32[]{:S(2)}) collective-permute-start(f32[4,7,256]{2,0,1:T(4,128)S(1)} %get-tuple-element.29), channel_id=1, source_target_pairs={{0,4},{4,8},{8,12},{12,16},{16,20},{20,24},{24,28},{28,32},{32,36}... | collective-permute-start | bytes 86024 | tf_op jit(solution)/shard_map/ppermute | solution.py:22
  46.0 16.4 %collective-permute-start.3 = (f32[4,7,256]{2,0,1:T(4,128)S(1)}, f32[4,7,256]{2,0,1:T(4,128)S(1)}, u32[]{:S(2)}, u32[]{:S(2)}) collective-permute-start(f32[4,7,256]{2,0,1:T(4,128)S(1)} %get-tuple-element.30), channel_id=1, source_target_pairs={{4,0},{8,4},{12,8},{16,12},{20,16},{24,20},{28,24},{32,28},{36,32}... | collective-permute-start | bytes 86024 | tf_op jit(solution)/shard_map/ppermute | solution.py:23
  70.6 21.1 %collective-permute-start.4 = (f32[4,7,256]{2,0,1:T(4,128)S(1)}, f32[4,7,256]{2,0,1:T(4,128)S(1)}, u32[]{:S(2)}, u32[]{:S(2)}) collective-permute-start(f32[4,7,256]{2,0,1:T(4,128)S(1)} %get-tuple-element.27), channel_id=1, source_target_pairs={{0,4},{4,8},{8,12},{12,16},{16,20},{20,24},{24,28},{28,32},{32,36}... | collective-permute-start | bytes 86024 | tf_op jit(solution)/shard_map/ppermute | solution.py:22
  76.3 15.5 %collective-permute-start.5 = (f32[4,7,256]{2,0,1:T(4,128)S(1)}, f32[4,7,256]{2,0,1:T(4,128)S(1)}, u32[]{:S(2)}, u32[]{:S(2)}) collective-permute-start(f32[4,7,256]{2,0,1:T(4,128)S(1)} %get-tuple-element.28), channel_id=1, source_target_pairs={{4,0},{8,4},{12,8},{16,12},{20,16},{24,20},{28,24},{32,28},{36,32}... | collective-permute-start | bytes 86024 | tf_op jit(solution)/shard_map/ppermute | solution.py:23
  100.0 23.7 %collective-permute-start.6 = (f32[4,7,256]{2,0,1:T(4,128)S(1)}, f32[4,7,256]{2,0,1:T(4,128)S(1)}, u32[]{:S(2)}, u32[]{:S(2)}) collective-permute-start(f32[4,7,256]{2,0,1:T(4,128)S(1)} %get-tuple-element.25), channel_id=1, source_target_pairs={{0,4},{4,8},{8,12},{12,16},{16,20},{20,24},{24,28},{28,32},{32,36}... | collective-permute-start | bytes 86024 | tf_op jit(solution)/shard_map/ppermute | solution.py:22
  106.9 16.8 %collective-permute-start.7 = (f32[4,7,256]{2,0,1:T(4,128)S(1)}, f32[4,7,256]{2,0,1:T(4,128)S(1)}, u32[]{:S(2)}, u32[]{:S(2)}) collective-permute-start(f32[4,7,256]{2,0,1:T(4,128)S(1)} %get-tuple-element.26), channel_id=1, source_target_pairs={{4,0},{8,4},{12,8},{16,12},{20,16},{24,20},{28,24},{32,28},{36,32}... | collective-permute-start | bytes 86024 | tf_op jit(solution)/shard_map/ppermute | solution.py:23
  225.4 8.4 %copy-start.3 = (f32[20,4]{0,1:T(4,128)}, f32[20,4]{0,1:T(4,128)S(1)}, u32[]{:S(2)}) copy-start(f32[20,4]{0,1:T(4,128)S(1)} %broadcast_multiply_fusion.1) | copy-start | bytes 964
where the time goes:
time: 320 us; the launch traced here: 319 us
  blocking collectives  218 us (68%)
  matrix products  53.8 us (17%)
  starting transfers between devices  29.2 us (9%)
  local copies, waits for them, and re-layouts  11.6 us (4%)
  other arithmetic  5.09 us (2%)
    psum x1, blocking collectives, shards(): proj = lax.psum(proj_part, ('space', 'inst')) / total_count  89.7 us
    psum x1, blocking collectives, shards(): gram = lax.psum(gram_part, ('space', 'inst')) / total_count  75 us
    all_gather x4, blocking collectives, derive(): lax.all_gather(field, 'inst', axis=0, tiled=True)  53.7 us
    dot_general x4, matrix products, operate(): jnp.einsum('flts,njls->fnjlt', onehot, layered, precision=lax.Precision.H...  23.2 us
    ppermute x4, starting transfers between devices, padded(): before = lax.ppermute(last, axis, up)  21.6 us
    dot_general x1, matrix products, shards(): jnp.einsum('bnjc,snjc->bs', basis, krylov, precision=lax.Precision.HIGHEST)  9.59 us
    ppermute x4, starting transfers between devices, padded(): after = lax.ppermute(initial, axis, down)  7.69 us
    dot_general x1, matrix products, shards(): jnp.einsum('bs,bnjc->snjc', proj, basis, precision=lax.Precision.HIGHEST)  7.59 us
  transfers between devices with their start and end apart: 8, of which 0 were waited for; matrix products, arithmetic and copies ran while one was open for 4% of the time, Pallas kernels for 0%

commit v1 on v0

v1 whole, which is shorter than its diff:
```python
import math

import jax
import jax.numpy as jnp
import numpy as np
from jax import lax
from jax.experimental import pallas as pl
from jax.experimental.pallas import tpu as pltpu
from jax.sharding import PartitionSpec as P

NT = 16
VARS = 7
NB = 20
S = 4
FACES = 6
FACE = 256
LAYERS = 8
NZ = NB + S
WIDE = 16
MESH = pl.DeviceIdType.MESH
F32 = jnp.float32
BF16 = jnp.bfloat16
TOTAL = float(NT * VARS * 131072)

GATHER = lax.GatherDimensionNumbers(
    offset_dims=(),
    collapsed_slice_dims=(1,),
    start_index_map=(1,),
    operand_batching_dims=(0,),
    start_indices_batching_dims=(0,),
)


def time_tables():
    n = np.arange(NT)
    diff = n[:, None] - n[None, :]
    angle = np.where(diff == 0, 1.0, np.pi * diff / NT)
    dmat = np.where(diff == 0, 0.0, 0.5 * (-1.0) ** diff * np.cos(angle) / np.sin(angle))
    tables = np.zeros((4, 8 * S, 8 * S))
    for d in range(4):
        for k in range(1, S + 1):
            for j in range(k):
                power = np.linalg.matrix_power(0.1 * dmat, k - j)
                part = math.comb(k, j) * power[:4, 4 * d : 4 * d + 4]
                for half in range(2):
                    r, c = (k - 1) * 8 + half * 4, j * 8 + half * 4
                    tables[d, r : r + 4, c : c + 4] = part
    high = tables.astype(jnp.bfloat16).astype(np.float64)
    low = (tables - high).astype(jnp.bfloat16).astype(np.float64)
    return np.concatenate([high, high, low], axis=2).astype(np.float32)


def take(x, index):
    return lax.gather(
        x, index[:, :, None], GATHER, slice_sizes=(1, 1), mode=lax.GatherScatterMode.PROMISE_IN_BOUNDS
    )


def kernel(
    start, coef, near, diag, basis, mixing, times,
    block, proj, factor,
    u, u4, w, bas, coef_own, near_own, diag_own, coef_side, near_side, diag_side,
    geo, seat, mix, acc, cf, slots,
    load_sem, ys, yr, xs, xr, gs, gr, out_sem, as_, ar,
):
    p, q = lax.axis_index("space"), lax.axis_index("inst")
    z, x, c = p // 8, (p // 2) % 4, p % 2
    has_low, has_high = p > 0, p < 63
    y_up, y_down = (q + 1) % 4, (q + 3) % 4

    def group_peer(phase, m):
        if phase == 0:
            return {"space": (z * 4 + m // 4) * 2 + c, "inst": m % 4}
        return {"space": ((m // 2) * 4 + x) * 2 + m % 2, "inst": q}

    mine = (x * 4 + q, z * 2 + c)

    loads = [
        pltpu.make_async_copy(coef, coef_own, load_sem.at[0]),
        pltpu.make_async_copy(near, near_own, load_sem.at[1]),
        pltpu.make_async_copy(diag, diag_own, load_sem.at[2]),
        pltpu.make_async_copy(start, u.at[0, 0, :, pl.ds(4, LAYERS)], load_sem.at[3]),
        pltpu.make_async_copy(basis, bas, load_sem.at[4]),
    ]
    for copy in loads:
        copy.start()

    barrier = pltpu.get_barrier_semaphore()

    def greet(phase):
        def body(i, carry):
            pl.semaphore_signal(
                barrier, inc=1, device_id=group_peer(phase, (mine[phase] + i) % 16), device_id_type=MESH
            )
            return carry

        lax.fori_loop(1, 16, body, 0)

    greet(0)
    greet(1)

    @pl.when(has_low)
    def _():
        pl.semaphore_signal(barrier, inc=1, device_id={"space": p - 1, "inst": q}, device_id_type=MESH)

    @pl.when(has_high)
    def _():
        pl.semaphore_signal(barrier, inc=1, device_id={"space": p + 1, "inst": q}, device_id_type=MESH)

    pl.semaphore_wait(barrier, 30 + jnp.where(has_low, 1, 0) + jnp.where(has_high, 1, 0))

    def y_copy(d, h):
        dst = u.at[0, d, :, pl.ds(4 + 4 * h, 4)]
        if d == 2:
            src = u.at[0, 3 if h == 0 else 1, :, pl.ds(4 + 4 * h, 4)]
            to = y_up if h == 0 else y_down
        else:
            src = start.at[:, pl.ds(4 * h, 4)]
            to = y_up if d == 3 else y_down
        return pltpu.make_async_remote_copy(
            src, dst, ys.at[d, h], yr.at[d, h], device_id={"space": p, "inst": to}, device_id_type=MESH
        )

    def x_copy(d, side):
        count = 4 if d == 0 else 3
        if side == 0:
            dst = u.at[0, d, :, pl.ds(4 - count, count)]
            src = start.at[:, pl.ds(8 - count, count)] if d == 0 else u.at[0, d, :, pl.ds(12 - count, count)]
            to = p + 1
        else:
            dst = u.at[0, d, :, pl.ds(12, count)]
            src = start.at[:, pl.ds(0, count)] if d == 0 else u.at[0, d, :, pl.ds(4, count)]
            to = p - 1
        return pltpu.make_async_remote_copy(
            src, dst, xs.at[d, side], xr.at[d, side], device_id={"space": to, "inst": q}, device_id_type=MESH
        )

    def side_copies(side):
        to = p + 1 if side == 0 else p - 1
        cut = pl.ds(5 * FACE, 3 * FACE) if side == 0 else pl.ds(0, 3 * FACE)
        pairs = (
            (coef.at[:, cut], coef_side.at[side]),
            (near.at[:, cut], near_side.at[side]),
            (diag, diag_side.at[side]),
        )
        return [
            pltpu.make_async_remote_copy(
                src, dst, gs.at[side, i], gr.at[side, i], device_id={"space": to, "inst": q}, device_id_type=MESH
            )
            for i, (src, dst) in enumerate(pairs)
        ]

    sends = (has_high, has_low)
    hears = (has_low, has_high)

    def x_start(d, side):
        @pl.when(sends[side])
        def _():
            x_copy(d, side).start()

    y_copy(3, 0).start()
    y_copy(1, 1).start()
    for side in range(2):

        @pl.when(sends[side])
        def _():
            for copy in side_copies(side):
                copy.start()

        x_start(0, side)
    y_copy(3, 1).start()
    y_copy(1, 0).start()

    for side in range(2):

        @pl.when(jnp.logical_not(hears[side]))
        def _():
            coef_side[side] = jnp.zeros((FACES, 3 * FACE), F32)
            near_side[side] = jnp.zeros((FACES, 3 * FACE), jnp.int32)
            diag_side[side] = jnp.zeros((16, 128), F32)
            for d in range(4):
                first = 0 if side == 0 else 12
                u[0, d, :, pl.ds(first, 4)] = jnp.zeros((VARS, 4, 8, 128), F32)

    sub = lax.broadcasted_iota(jnp.int32, (8, 128), 0)
    lane = lax.broadcasted_iota(jnp.int32, (8, 128), 1)
    upper = sub >= 4

    for i in range(VARS):
        for j in range(VARS):
            mix[i * VARS + j] = jnp.full((8, 128), mixing[i, j], F32)

    for copy in loads[:3]:
        copy.wait()

    def spread(values, at):
        first = jnp.broadcast_to(values[:, at : at + 128], (8, 128))
        second = jnp.broadcast_to(values[:, at + 128 : at + 256], (8, 128))
        return jnp.where(upper, second, first)

    def place(layer, coefs, nears, at, diags):
        total = None
        for f in range(FACES):
            value = spread(coefs[f : f + 1], at)
            geo[1 + f, layer] = value
            total = value if total is None else total + value
        geo[0, layer] = total
        geo[7, layer] = jnp.where(
            upper, jnp.broadcast_to(diags[1:2], (8, 128)), jnp.broadcast_to(diags[0:1], (8, 128))
        )
        for f in range(2, FACES):
            seat[f - 2, layer] = spread(nears[f : f + 1], at) & (FACE - 1)

    coefs, nears, diags = coef_own[...], near_own[...], diag_own[...]
    for layer in range(LAYERS):
        place(4 + layer, coefs, nears, layer * FACE, diags[2 * layer : 2 * layer + 2])
    for side in range(2):

        @pl.when(hears[side])
        def _():
            for copy in side_copies(side):
                copy.wait_recv()

        coefs, nears, diags = coef_side[side], near_side[side], diag_side[side]
        for layer in range(3):
            first = 10 + 2 * layer if side == 0 else 2 * layer
            place((1 if side == 0 else 12) + layer, coefs, nears, layer * FACE, diags[first : first + 2])

    def step(src, dst, low, high):
        def pair(i, carry):
            a = low + 2 * i
            values, fluxes = [], []
            for e in range(2):
                g = [geo[f, a + e] for f in range(7)]
                lanes, same = [], []
                for f in range(4):
                    seats = seat[f, a + e]
                    lanes.append(seats & 127)
                    same.append((seats >= 128) == upper)
                for v in range(VARS):
                    center = src[v, a + e]
                    other = pltpu.roll(center, 4, 0)
                    flux = g[0] * center - g[1] * src[v, a + e - 1] - g[2] * src[v, a + e + 1]
                    for f in range(4):
                        value = jnp.where(same[f], take(center, lanes[f]), take(other, lanes[f]))
                        flux = flux - g[3 + f] * value
                    fluxes.append(flux)
            d0, d1 = geo[7, a], geo[7, a + 1]
            for i in range(VARS):
                r0, r1 = d0 * src[i, a], d1 * src[i, a + 1]
                for j in range(VARS):
                    m = mix[i * VARS + j]
                    r0 = r0 + m * fluxes[j]
                    r1 = r1 + m * fluxes[VARS + j]
                dst[i, a], dst[i, a + 1] = r0, r1
            return carry

        lax.fori_loop(0, (high - low) // 2, pair, 0)

    def chain(d):
        low = 1 if d == 0 else 2
        for j in range(3):
            step(u.at[j, d], u.at[j + 1, d], low + j, 16 - low - j)
        if d == 0:
            step(u.at[3, 0], u4, 4, 12)

    def combine(d):
        table = times[d].astype(BF16)

        def body(i, carry):
            v, l = i // 4, 2 * (i % 4)
            columns = []
            for e in range(2):
                parts = jnp.concatenate([u[j, d, v, 4 + l + e] for j in range(S)], axis=0)
                high = parts.astype(BF16)
                low = (parts - high.astype(F32)).astype(BF16)
                columns.append(jnp.concatenate([high, low, high], axis=0))
            out = jnp.dot(table, jnp.concatenate(columns, axis=1), preferred_element_type=F32)
            for e in range(2):
                for k in range(S):
                    term = out[8 * k : 8 * k + 8, 128 * e : 128 * e + 128]
                    if d == 0:
                        last = u4[v, 4 + l + e] if k == S - 1 else u[k + 1, 0, v, 4 + l + e]
                        w[k, v, l + e] = last + term
                    else:
                        w[k, v, l + e] += term
            return carry

        lax.fori_loop(0, VARS * 4, body, 0)

    def products(left, right, pairs, places):
        def body(i, sums):
            v, l = i // LAYERS, i % LAYERS
            a = {k: r[n, v, l] for k, (r, n) in left.items()}
            b = {k: r[n, v, l] for k, (r, n) in right.items()}
            return tuple(s + a[m] * b[n] for s, (m, n) in zip(sums, pairs))

        zero = jnp.zeros((8, 128), F32)
        sums = lax.fori_loop(0, VARS * LAYERS, body, (zero,) * len(pairs))
        for total, spots in zip(sums, places):
            for row, column in spots:
                acc[pl.ds((column * NZ + row) * 8, 8)] = total

    def basis_block(i, j):
        pairs = [(a, b) for a in range(5 * i, 5 * i + 5) for b in range(5 * j, 5 * j + 5) if a <= b]
        products(
            {a: (bas, a) for a in range(5 * i, 5 * i + 5)},
            {b: (bas, b) for b in range(5 * j, 5 * j + 5)},
            pairs,
            [((a, b), (b, a)) if a != b else ((a, b),) for a, b in pairs],
        )

    def gather_sums(columns):
        wide = lax.broadcasted_iota(jnp.int32, (NZ, 128), 1)
        result = jnp.zeros((NZ, 128), F32)
        for column in columns:
            rows = acc[pl.ds(column * NZ * 8, NZ, stride=8)]
            for s in range(1, 8):
                rows = rows + acc[pl.ds(column * NZ * 8 + s, NZ, stride=8)]
            result = jnp.where(wide == column, jnp.sum(rows, axis=1, keepdims=True), result)
        return result

    def x_wait(d):
        for side in range(2):

            @pl.when(hears[side])
            def _():
                x_copy(d, side).wait_recv()

    loads[3].wait()
    x_wait(0)
    chain(0)
    combine(0)

    y_copy(3, 0).wait_recv()
    y_copy(2, 0).start()
    y_copy(1, 1).wait_recv()
    y_copy(2, 1).start()
    x_start(3, 1)
    x_start(1, 0)

    loads[4].wait()
    todo = [(i, j) for i in range(4) for j in range(i, 4)]
    for i, j in todo[:4]:
        basis_block(i, j)

    y_copy(3, 1).wait_recv()
    x_start(3, 0)
    y_copy(1, 0).wait_recv()
    x_start(1, 1)

    for i, j in todo[4:]:
        basis_block(i, j)
    sums = gather_sums(range(NB))

    y_copy(2, 0).wait_recv()
    x_start(2, 1)
    y_copy(2, 1).wait_recv()
    x_start(2, 0)

    for d in (3, 1, 2):
        x_wait(d)
        chain(d)
        combine(d)

    for first in (0, 2):
        new = range(first, first + 2)
        pairs = [(b, k) for k in new for b in range(NB)]
        spots = [((b, NB + k),) for b, k in pairs]
        extra = [(NB + first, first), (NB + first, first + 1), (NB + first + 1, first + 1)]
        if first == 2:
            extra += [(NB + t, k) for t in range(2) for k in new]
        pairs = pairs + extra
        spots = spots + [
            ((t, NB + k), (NB + k, t)) if t != NB + k else ((t, t),) for t, k in extra
        ]
        left = {b: (bas, b) for b in range(NB)}
        left.update({NB + t: (w, t) for t in range(first + 2)})
        products(left, {k: (w, k) for k in new}, pairs, spots)

    wide_row = lax.broadcasted_iota(jnp.int32, (NZ, 128), 0)
    wide_lane = lax.broadcasted_iota(jnp.int32, (NZ, 128), 1)
    sums = jnp.where(wide_row < NB, sums, 0.0)
    sums = jnp.where(wide_lane >= NB, gather_sums(range(NB, NZ)), sums)
    sums = jnp.where(wide_lane < NZ, sums, 0.0)
    packed = jnp.where(
        lane < 32,
        sums[0:8],
        jnp.where(lane < 64, pltpu.roll(sums[8:16], 32, 1), pltpu.roll(sums[16:24], 64, 1)),
    )

    def exchange(phase, value):
        me = mine[phase]
        slots[phase, me] = value

        def copy(to, spot):
            return pltpu.make_async_remote_copy(
                slots.at[phase, me],
                slots.at[phase, spot],
                as_.at[phase, to],
                ar.at[phase, spot],
                device_id=group_peer(phase, to),
                device_id_type=MESH,
            )

        def send(i, carry):
            copy((me + i) % 16, me).start()
            return carry

        def receive(i, carry):
            other = (me + i) % 16
            copy(other, other).wait_recv()
            return carry

        lax.fori_loop(1, 16, send, 0)
        lax.fori_loop(1, 16, receive, 0)
        total = slots[phase, 0]
        for m in range(1, 16):
            total = total + slots[phase, m]

        def sent(i, carry):
            copy((me + i) % 16, me).wait_send()
            return carry

        return total, lambda: lax.fori_loop(1, 16, sent, 0)

    packed, drain0 = exchange(0, packed)
    packed, drain1 = exchange(1, packed)

    packed = packed / TOTAL
    means = jnp.concatenate([packed, pltpu.roll(packed, 96, 1), pltpu.roll(packed, 64, 1)], axis=0)
    column = pltpu.roll(means, 128 - NB, 1)
    proj[...] = column[0:NB, 0:S]
    coefs = jnp.where(jnp.logical_and(wide_row < NB, wide_lane < S), column, 0.0)
    twice = -2.0 * coefs
    for b in range(NB):
        twice = twice + jnp.where(wide_row < NB, means[:, b : b + 1], 0.0) * coefs[b : b + 1]
    gram = []
    for s in range(S):
        row = jnp.sum(coefs[:, s : s + 1] * twice, axis=0, keepdims=True) + column[NB + s : NB + s + 1]
        gram.append([jnp.broadcast_to(row[:, t : t + 1], (8, 128)) for t in range(S)])

    lower = [[None] * S for _ in range(S)]
    inverse = [[None] * S for _ in range(S)]
    for j in range(S):
        value = gram[j][j]
        for k in range(j):
            value = value - lower[j][k] * lower[j][k]
        lower[j][j] = jnp.sqrt(value)
        inverse[j][j] = 1.0 / lower[j][j]
        for i in range(j + 1, S):
            value = gram[i][j]
            for k in range(j):
                value = value - lower[i][k] * lower[j][k]
            lower[i][j] = value * inverse[j][j]
    for j in range(S):
        for i in range(j + 1, S):
            value = lower[i][j] * inverse[j][j]
            for k in range(j + 1, i):
                value = value + lower[i][k] * inverse[k][j]
            inverse[i][j] = -inverse[i][i] * value
    upper_factor = jnp.zeros((8, 128), F32)
    for s in range(S):
        for t in range(s + 1):
            upper_factor = jnp.where(jnp.logical_and(sub == t, lane == s), lower[s][t], upper_factor)
    factor[...] = upper_factor[0:S, 0:S]

    for s in range(S):
        value = None
        for t in range(s + 1):
            term = jnp.broadcast_to(coefs[:, t : t + 1], (NZ, 128)) * inverse[s][t][0:1]
            value = term if value is None else value + term
        cf[s] = -value
        for t in range(s + 1):
            cf[s, NB + t : NB + t + 1] = inverse[s][t][0:1]

    def out_copy(v):
        return pltpu.make_async_copy(w.at[:, v], block.at[:, v], out_sem.at[v])

    def finish(v, carry):
        def weight(s, n):
            return jnp.broadcast_to(cf[s, n : n + 1], (8, 128))

        totals = [[None] * LAYERS for _ in range(S)]
        for n in range(NZ):
            vectors = [(w[n - NB, v, l] if n >= NB else bas[n, v, l]) for l in range(LAYERS)]
            for s in range(S):
                if n >= NB and n - NB > s:
                    continue
                m = weight(s, n)
                for l in range(LAYERS):
                    term = m * vectors[l]
                    totals[s][l] = term if totals[s][l] is None else totals[s][l] + term
        for s in range(S):
            for l in range(LAYERS):
                w[s, v, l] = totals[s][l]
        out_copy(v).start()
        return carry

    lax.fori_loop(0, VARS, finish, 0)

    drain0()
    drain1()
    for d in range(4):
        for h in range(2):
            if d > 0:
                y_copy(d, h).wait_send()

            @pl.when(sends[h])
            def _():
                x_copy(d, h).wait_send()

    for side in range(2):

        @pl.when(sends[side])
        def _():
            for copy in side_copies(side):
                copy.wait_send()

    def landed(v, carry):
        out_copy(v).wait()
        return carry

    lax.fori_loop(0, VARS, landed, 0)


def shards(start, shifted_diag, face_coef, mixing, neighbours, basis):
    view = start.reshape(4, VARS, LAYERS, 2, 128).transpose(1, 2, 3, 0, 4).reshape(VARS, LAYERS, 8, 128)
    vectors = basis.reshape(NB, 4, VARS, LAYERS, 2, 128).transpose(0, 2, 3, 4, 1, 5)
    vectors = vectors.reshape(NB, VARS, LAYERS, 8, 128)
    hbm = pl.BlockSpec(memory_space=pl.ANY)
    vmem = pl.BlockSpec(memory_space=pltpu.VMEM)
    dma = pltpu.SemaphoreType.DMA
    block, proj, factor = pl.pallas_call(
        kernel,
        out_shape=(
            jax.ShapeDtypeStruct((S, VARS, LAYERS, 8, 128), F32),
            jax.ShapeDtypeStruct((NB, S), F32),
            jax.ShapeDtypeStruct((S, S), F32),
        ),
        in_specs=[hbm, hbm, hbm, hbm, hbm, pl.BlockSpec(memory_space=pltpu.SMEM), vmem],
        out_specs=(hbm, vmem, vmem),
        scratch_shapes=[
            pltpu.VMEM((4, 4, VARS, WIDE, 8, 128), F32),
            pltpu.VMEM((VARS, WIDE, 8, 128), F32),
            pltpu.VMEM((S, VARS, LAYERS, 8, 128), F32),
            pltpu.VMEM((NB, VARS, LAYERS, 8, 128), F32),
            pltpu.VMEM((FACES, LAYERS * FACE), F32),
            pltpu.VMEM((FACES, LAYERS * FACE), jnp.int32),
            pltpu.VMEM((16, 128), F32),
            pltpu.VMEM((2, FACES, 3 * FACE), F32),
            pltpu.VMEM((2, FACES, 3 * FACE), jnp.int32),
            pltpu.VMEM((2, 16, 128), F32),
            pltpu.VMEM((8, WIDE, 8, 128), F32),
            pltpu.VMEM((4, WIDE, 8, 128), jnp.int32),
            pltpu.VMEM((VARS * VARS, 8, 128), F32),
            pltpu.VMEM((NZ * NZ * 8, 128), F32),
            pltpu.VMEM((S, NZ, 128), F32),
            pltpu.VMEM((2, 16, 8, 128), F32),
            dma((5,)),
            dma((4, 2)),
            dma((4, 2)),
            dma((4, 2)),
            dma((4, 2)),
            dma((2, 3)),
            dma((2, 3)),
            dma((VARS,)),
            dma((2, 16)),
            dma((2, 16)),
        ],
        compiler_params=pltpu.CompilerParams(
            collective_id=0, has_side_effects=True, vmem_limit_bytes=40 * 1024 * 1024
        ),
        name="krylov_block",
    )(view, face_coef, neighbours, shifted_diag.reshape(16, 128), vectors, mixing, jnp.asarray(time_tables()))
    block = block.reshape(S, VARS, LAYERS, 2, 4, 128).transpose(0, 4, 1, 2, 3, 5)
    return block.reshape(S, 4, VARS, LAYERS * FACE), proj, factor


def solution(mesh):
    return jax.shard_map(
        shards,
        mesh=mesh,
        in_specs=(
            P("inst", None, "space"),
            P("space"),
            P(None, "space"),
            P(),
            P(None, "space"),
            P(None, "inst", None, "space"),
        ),
        out_specs=(P(None, "inst", None, "space"), P(), P()),
        check_vma=False,
    )
```

time: 320 us -> 95.1 us (0.30)
  blocking collectives: 218 us -> 0 us
  Pallas kernels: 0 us -> 84.8 us
  matrix products: 53.8 us -> 0 us
  starting transfers between devices: 29.2 us -> 0 us
  other arithmetic: 5.09 us -> 0 us
    psum x2 -> x0, blocking collectives: 165 us -> none  [the longest x1 89.7 us: shards(): proj = lax.psum(proj_part, ('space', 'inst')) / total_count]
    pallas_call x0 -> x1, Pallas kernels: none -> 84.8 us  [shards(): pl.pallas_call(kernel, out_shape=(jax.ShapeDtypeStruct((S, VARS, LAYERS,...]
    all_gather x4 -> x0, blocking collectives: 53.7 us -> none  [derive(): lax.all_gather(field, 'inst', axis=0, tiled=True)]
    dot_general x16 -> x0, matrix products: 53.6 us -> none  [the longest x4 23.2 us: operate(): jnp.einsum('flts,njls->fnjlt', onehot, layered, precision=lax.Precision.H...]
    ppermute x8 -> x0, starting transfers between devices: 29.2 us -> none  [the longest x4 21.6 us: padded(): before = lax.ppermute(last, axis, up)]
    unnamed x11 -> x17, local copies, waits for them, and re-layouts: 3.29 us -> 9.29 us
    slice x25 -> x0, local copies, waits for them, and re-layouts: 4.61 us -> none  [the longest x20 2.69 us: operate(): flux = flux + coefficients[face] * (middle - within_vals[face - 2])]
  transfers between devices with their start and end apart: 8 -> 0, of which waited for: 0 -> 0; matrix products, arithmetic and copies ran while one was open for 4% -> 0% of each run, Pallas kernels for 0% -> 0%
where the time goes in v1:
time: 95.1 us; the launch traced here: 94.8 us
  Pallas kernels  84.8 us (89%)
  local copies, waits for them, and re-layouts  9.29 us (10%)
    pallas_call x1, Pallas kernels, shards(): pl.pallas_call(kernel, out_shape=(jax.ShapeDtypeStruct((S, VARS, LAYERS,...  84.8 us
    unnamed x17, local copies, waits for them, and re-layouts  9.29 us

profile of v1, /device:TPU:1, one launch (start us, length us, event | category | flops | bytes accessed | tf_op | source)
XLA Modules:
  0.0 94.8 jit_solution(4420531886803532251)
XLA Ops:
  0.6 0.0 copy-start
  0.6 2.3 %copy-done = f32[20,4,7,2048]{3,1,2,0:T(4,128)S(1)} copy-done((f32[20,4,7,2048]{3,1,2,0:T(4,128)S(1)}, f32[20,4,7,2048]{3,1,2,0:T(4,128)}, u32[]{:S(2)}) %copy-start) | copy-done | bytes 4587544
  2.9 0.0 copy-start.1
  2.9 0.9 copy-done.1
  3.9 0.0 copy-start.2
  3.9 0.8 copy-done.2
  4.7 0.0 copy-start.3
  4.7 0.8 copy-done.3
  5.6 0.0 copy-start.4
  5.6 0.8 copy-done.4
  6.4 0.0 copy-start.5
  6.4 0.7 copy-done.5
  7.1 0.0 copy-start.6
  7.1 0.7 copy-done.6
  7.8 84.8 %krylov_block.1 = (f32[4,7,8,8,128]{4,3,2,1,0:T(8,128)S(1)}, f32[20,4]{1,0:T(8,128)S(1)}, f32[4,4]{1,0:T(4,128)S(1)}) custom-call(f32[7,8,8,128]{3,2,1,0:T(8,128)S(1)} %bitcast.18, f32[6,2048]{1,0:T(8,128)S(1)} %copy-done.2, s32[6,2048]{1,0:T(8,128)S(1)} %copy-done.3, f32[16,128]{1,0:T(8,128)S(1)} %bitcast.19, f32[20,7,8,8,128]{4,3,2,1,0:T(8,128)S(1)} %bitcast.16, ...), custom_call_target="tpu_custom_call" | custom-call | tf_op jit(solution)/shard_map/krylov_block/pallas_call | solution.py:534
  92.6 0.7 copy.13
  93.3 0.9 copy.16
  94.2 0.6 copy.17
Async XLA Ops:
  0.6 2.3 %copy-start = (f32[20,4,7,2048]{3,1,2,0:T(4,128)S(1)}, f32[20,4,7,2048]{3,1,2,0:T(4,128)}, u32[]{:S(2)}) copy-start(f32[20,4,7,2048]{3,1,2,0:T(4,128)} %param.12) | copy-start | bytes 13762564
  2.9 0.9 copy-start.1
  3.9 0.8 copy-start.2
  4.7 0.8 copy-start.3
  5.6 0.8 copy-start.4
  6.4 0.7 copy-start.5
  7.1 0.7 copy-start.6

commit v2 on v1

v2 whole, which is shorter than its diff:
```python
import math

import jax
import jax.numpy as jnp
import numpy as np
from jax import lax
from jax.experimental import pallas as pl
from jax.experimental.pallas import tpu as pltpu
from jax.sharding import PartitionSpec as P

NT = 16
VARS = 7
NB = 20
S = 4
FACES = 6
FACE = 256
LAYERS = 8
NZ = NB + S
WIDE = 16
MESH = pl.DeviceIdType.MESH
F32 = jnp.float32
BF16 = jnp.bfloat16
UNITS = 14
TOTAL = float(NT * VARS * 131072)


def time_tables():
    n = np.arange(NT)
    diff = n[:, None] - n[None, :]
    angle = np.where(diff == 0, 1.0, np.pi * diff / NT)
    dmat = np.where(diff == 0, 0.0, 0.5 * (-1.0) ** diff * np.cos(angle) / np.sin(angle))
    tables = np.zeros((4, 8 * S, 8 * S))
    for d in range(4):
        for k in range(1, S + 1):
            for j in range(k):
                power = np.linalg.matrix_power(0.1 * dmat, k - j)
                part = math.comb(k, j) * power[:4, 4 * d : 4 * d + 4]
                for half in range(2):
                    r, c = (k - 1) * 8 + half * 4, j * 8 + half * 4
                    tables[d, r : r + 4, c : c + 4] = part
    high = tables.astype(jnp.bfloat16).astype(np.float64)
    low = (tables - high).astype(jnp.bfloat16).astype(np.float64)
    return np.concatenate([high, high, low], axis=2).astype(np.float32)


def kernel(
    start, coef, near, diag, basis, mixing, times,
    krylov, products_out,
    u, u4, w, bas, coef_own, near_own, diag_own, coef_side, near_side, diag_side,
    mixing_own, tables, geo, weights, mix, sums, slots,
    load_sem, ys, yr, xs, xr, gs, gr, as_, ar, out_sem,
):
    p, q = lax.axis_index("space"), lax.axis_index("inst")
    z, x, c = p // 8, (p // 2) % 4, p % 2
    has_low, has_high = p > 0, p < 63
    y_up, y_down = (q + 1) % 4, (q + 3) % 4

    def group_peer(phase, m):
        if phase == 0:
            return {"space": (z * 4 + m // 4) * 2 + c, "inst": m % 4}
        return {"space": ((m // 2) * 4 + x) * 2 + m % 2, "inst": q}

    mine = (x * 4 + q, z * 2 + c)

    loads = [
        pltpu.make_async_copy(coef, coef_own, load_sem.at[0]),
        pltpu.make_async_copy(near, near_own, load_sem.at[1]),
        pltpu.make_async_copy(diag, diag_own, load_sem.at[2]),
        pltpu.make_async_copy(mixing, mixing_own, load_sem.at[3]),
        pltpu.make_async_copy(start, u.at[0, 0, :, pl.ds(4, LAYERS)], load_sem.at[4]),
        pltpu.make_async_copy(times, tables, load_sem.at[5]),
        pltpu.make_async_copy(basis, bas, load_sem.at[6]),
    ]
    for copy in loads:
        copy.start()

    barrier = pltpu.get_barrier_semaphore()

    def greet(phase):
        def body(i, carry):
            pl.semaphore_signal(
                barrier, inc=1, device_id=group_peer(phase, (mine[phase] + i) % 16), device_id_type=MESH
            )
            return carry

        lax.fori_loop(1, 16, body, 0)

    greet(0)
    greet(1)

    @pl.when(has_low)
    def _():
        pl.semaphore_signal(barrier, inc=1, device_id={"space": p - 1, "inst": q}, device_id_type=MESH)

    @pl.when(has_high)
    def _():
        pl.semaphore_signal(barrier, inc=1, device_id={"space": p + 1, "inst": q}, device_id_type=MESH)

    pl.semaphore_wait(barrier, 30 + jnp.where(has_low, 1, 0) + jnp.where(has_high, 1, 0))

    def y_copy(d, h):
        dst = u.at[0, d, :, pl.ds(4 + 4 * h, 4)]
        if d == 2:
            src = u.at[0, 3 if h == 0 else 1, :, pl.ds(4 + 4 * h, 4)]
            to = y_up if h == 0 else y_down
        else:
            src = start.at[:, pl.ds(4 * h, 4)]
            to = y_up if d == 3 else y_down
        return pltpu.make_async_remote_copy(
            src, dst, ys.at[d, h], yr.at[d, h], device_id={"space": p, "inst": to}, device_id_type=MESH
        )

    def x_copy(d, side):
        count = 4 if d == 0 else 3
        if side == 0:
            dst = u.at[0, d, :, pl.ds(4 - count, count)]
            src = start.at[:, pl.ds(8 - count, count)] if d == 0 else u.at[0, d, :, pl.ds(12 - count, count)]
            to = p + 1
        else:
            dst = u.at[0, d, :, pl.ds(12, count)]
            src = start.at[:, pl.ds(0, count)] if d == 0 else u.at[0, d, :, pl.ds(4, count)]
            to = p - 1
        return pltpu.make_async_remote_copy(
            src, dst, xs.at[d, side], xr.at[d, side], device_id={"space": to, "inst": q}, device_id_type=MESH
        )

    def side_copies(side):
        to = p + 1 if side == 0 else p - 1
        cut = pl.ds(5 * FACE, 3 * FACE) if side == 0 else pl.ds(0, 3 * FACE)
        pairs = (
            (coef.at[:, cut], coef_side.at[side]),
            (near.at[:, cut], near_side.at[side]),
            (diag, diag_side.at[side]),
        )
        return [
            pltpu.make_async_remote_copy(
                src, dst, gs.at[side, i], gr.at[side, i], device_id={"space": to, "inst": q}, device_id_type=MESH
            )
            for i, (src, dst) in enumerate(pairs)
        ]

    sends = (has_high, has_low)
    hears = (has_low, has_high)

    def x_start(d, side):
        @pl.when(sends[side])
        def _():
            x_copy(d, side).start()

    y_copy(3, 0).start()
    y_copy(1, 1).start()
    for side in range(2):

        @pl.when(sends[side])
        def _():
            for copy in side_copies(side):
                copy.start()

        x_start(0, side)
    y_copy(3, 1).start()
    y_copy(1, 0).start()

    for side in range(2):

        @pl.when(jnp.logical_not(hears[side]))
        def _():
            coef_side[side] = jnp.zeros((FACES, 3 * FACE), F32)
            near_side[side] = jnp.zeros((FACES, 3 * FACE), jnp.int32)
            diag_side[side] = jnp.zeros((16, 128), F32)
            for d in range(4):
                first = 0 if side == 0 else 12
                u[0, d, :, pl.ds(first, 4)] = jnp.zeros((VARS, 4, 8, 128), F32)

    sub = lax.broadcasted_iota(jnp.int32, (8, 128), 0)
    lane = lax.broadcasted_iota(jnp.int32, (8, 128), 1)
    upper = sub >= 4

    for copy in loads[:4]:
        copy.wait()

    matrix = mixing_own[...]
    for i in range(VARS):
        for j in range(VARS):
            mix[i * VARS + j] = jnp.broadcast_to(matrix[i : i + 1, j : j + 1], (8, 128))

    def spread(values, at):
        first = jnp.broadcast_to(values[:, at : at + 128], (8, 128))
        second = jnp.broadcast_to(values[:, at + 128 : at + 256], (8, 128))
        return jnp.where(upper, second, first)

    source = lax.broadcasted_iota(jnp.int32, (32, FACE), 0)

    def place(layer, coefs, nears, at, diags):
        values = [spread(coefs[f : f + 1], at) for f in range(FACES)]
        geo[0, layer] = sum(values[1:], values[0])
        geo[1, layer], geo[2, layer] = values[0], values[1]
        geo[3, layer] = jnp.where(
            upper, jnp.broadcast_to(diags[1:2], (8, 128)), jnp.broadcast_to(diags[0:1], (8, 128))
        )
        rows = [
            (nears[f : f + 1, at : at + FACE] & (FACE - 1), coefs[f : f + 1, at : at + FACE])
            for f in range(2, FACES)
        ]

        for r in range(0, FACE, 32):
            total = None
            for cells, values in rows:
                term = jnp.where(source + r == cells, values, 0.0)
                total = term if total is None else total + term
            high = total.astype(BF16)
            weights[layer, 0, pl.ds(r, 32)] = high
            weights[layer, 1, pl.ds(r, 32)] = (total - high.astype(F32)).astype(BF16)

    coefs, nears, diags = coef_own[...], near_own[...], diag_own[...]
    for layer in range(LAYERS):
        place(4 + layer, coefs, nears, layer * FACE, diags[2 * layer : 2 * layer + 2])
    for side in range(2):

        @pl.when(hears[side])
        def _():
            for copy in side_copies(side):
                copy.wait_recv()

        coefs, nears, diags = coef_side[side], near_side[side], diag_side[side]
        for layer in range(3):
            first = 10 + 2 * layer if side == 0 else 2 * layer
            place((1 if side == 0 else 12) + layer, coefs, nears, layer * FACE, diags[first : first + 2])

    def within(groups, layer):
        rows = []
        for values in groups:
            for i in range(0, VARS, 2):
                one = values[i]
                two = values[min(i + 1, VARS - 1)]
                first = jnp.where(upper, pltpu.roll(two, 4, 0), one)
                second = jnp.where(upper, two, pltpu.roll(one, 4, 0))
                rows.append(jnp.concatenate([first, second], axis=1))
        rows = jnp.concatenate(rows, axis=0)
        count = rows.shape[0]
        high = rows.astype(BF16)
        low = (rows - high.astype(F32)).astype(BF16)
        both = jnp.dot(jnp.concatenate([high, low], axis=0), weights[layer, 0], preferred_element_type=F32)
        out = both[0:count] + both[count:] + jnp.dot(high, weights[layer, 1], preferred_element_type=F32)
        results = []
        for at in range(0, count, 32):
            result = []
            for i in range(0, VARS, 2):
                first, second = (out[at + 4 * i : at + 4 * i + 8, e : e + 128] for e in (0, 128))
                if i + 1 == VARS:
                    result.append(jnp.where(upper, second, first))
                else:
                    result.append(jnp.where(upper, pltpu.roll(second, 4, 0), first))
                    result.append(jnp.where(upper, second, pltpu.roll(first, 4, 0)))
            results.append(result)
        return results

    def step(pairs, low, high):
        count = max(n for n in range(1, UNITS // len(pairs) + 1) if (high - low) % n == 0)

        def body(i, carry):
            layers = [low + count * i + e for e in range(count)]
            fluxes = []
            for b in layers:
                centers = [[src[v, b] for v in range(VARS)] for src, _ in pairs]
                inner = within(centers, b)
                g = [geo[f, b] for f in range(3)]
                for (src, _), center, inside in zip(pairs, centers, inner):
                    fluxes.append(
                        [
                            g[0] * center[v] - g[1] * src[v, b - 1] - g[2] * src[v, b + 1] - inside[v]
                            for v in range(VARS)
                        ]
                    )
            units = [(src, dst, b) for b in layers for src, dst in pairs]
            for i in range(VARS):
                totals = [geo[3, b] * src[i, b] for src, _, b in units]
                for j in range(VARS):
                    m = mix[i * VARS + j]
                    totals = [t + m * flux[j] for t, flux in zip(totals, fluxes)]
                for (_, dst, b), total in zip(units, totals):
                    dst[i, b] = total
            return carry

        lax.fori_loop(0, (high - low) // count, body, 0)

    def chain(*groups):
        low = 1 if groups[0] == 0 else 2
        for j in range(3):
            step([(u.at[j, d], u.at[j + 1, d]) for d in groups], low + j, 16 - low - j)
        if groups[0] == 0:
            step([(u.at[3, 0], u4)], 4, 12)

    def combine(*groups):
        table = jnp.concatenate([tables[d] for d in groups], axis=1).astype(BF16)
        for v in range(VARS):
            stack = []
            for d in groups:
                parts = jnp.concatenate(
                    [jnp.concatenate([u[j, d, v, 4 + l] for l in range(LAYERS)], axis=1) for j in range(S)],
                    axis=0,
                )
                high = parts.astype(BF16)
                low = (parts - high.astype(F32)).astype(BF16)
                stack += [high, low, high]
            out = jnp.dot(table, jnp.concatenate(stack, axis=0), preferred_element_type=F32)
            for l in range(LAYERS):
                for k in range(S):
                    term = out[8 * k : 8 * k + 8, 128 * l : 128 * l + 128]
                    if groups[0] == 0:
                        last = u4[v, 4 + l] if k == S - 1 else u[k + 1, 0, v, 4 + l]
                        w[k, v, l] = last + term
                    else:
                        w[k, v, l] += term

    bits = {k: (sub // k) % 2 == 1 for k in (1, 2, 4)}
    zero = jnp.zeros((8, 128), F32)

    def merge(parts):
        for k in (1, 2, 4):
            parts = [
                jnp.where(bits[k], b, a) + pltpu.roll(jnp.where(bits[k], a, b), k, 0)
                for a, b in zip(parts[::2], parts[1::2])
            ]
        return parts[0]

    def products(left, right, pairs):
        def body(v, totals):
            totals = list(totals)
            for l in range(LAYERS):
                a = {k: r[n, v, l] for k, (r, n) in left.items()}
                b = {k: r[n, v, l] for k, (r, n) in right.items()}
                totals = [t + a[m] * b[n] for t, (m, n) in zip(totals, pairs)]
            return tuple(totals)

        totals = lax.fori_loop(0, VARS, body, (zero,) * len(pairs))
        return dict(zip(pairs, totals))

    def basis_block(i, j):
        rows = range(8 * i, min(8 * i + 8, NB))
        columns = range(5 * j, 5 * j + 5)
        totals = products(
            {a: (bas, a) for a in rows},
            {b: (bas, b) for b in columns},
            [(a, b) for a in rows for b in columns if a <= b],
        )
        for b in columns:
            sums[b, pl.ds(8 * i, 8)] = merge([totals.get((a, b), zero) for a in range(8 * i, 8 * i + 8)])

    wide_row = lax.broadcasted_iota(jnp.int32, (NZ, 128), 0)
    wide_lane = lax.broadcasted_iota(jnp.int32, (NZ, 128), 1)

    def merge_lanes(columns):
        parts = [columns.get(i) for i in range(32)]
        for k in (1, 2, 4, 8, 16):
            bit = (lane // k) % 2 == 1
            merged = []
            for a, b in zip(parts[::2], parts[1::2]):
                if a is None and b is None:
                    merged.append(None)
                    continue
                a, b = zero if a is None else a, zero if b is None else b
                merged.append(jnp.where(bit, b, a) + pltpu.roll(jnp.where(bit, a, b), k, 1))
            parts = merged
        total = parts[0]
        total = total + pltpu.roll(total, 32, 1)
        return total + pltpu.roll(total, 64, 1)

    column_of = lane % 32

    def basis_sums():
        result = []
        for i in range(3):
            part = merge_lanes({b: sums[b, pl.ds(8 * i, 8)] for b in range(8 * i, NB)})
            part = jnp.where(sub + 8 * i <= column_of, part, 0.0)
            part = jnp.where(sub + 8 * i == column_of, 0.5 * part, part)
            result.append(jnp.where(column_of < NB, part, 0.0))
        return result

    def x_wait(d):
        for side in range(2):

            @pl.when(hears[side])
            def _():
                x_copy(d, side).wait_recv()

    loads[4].wait()
    loads[5].wait()
    x_wait(0)
    chain(0)
    combine(0)

    y_copy(3, 0).wait_recv()
    y_copy(2, 0).start()
    y_copy(1, 1).wait_recv()
    y_copy(2, 1).start()
    x_start(3, 1)
    x_start(1, 0)

    loads[6].wait()
    for i, j in ((0, 0), (0, 1), (0, 2)):
        basis_block(i, j)

    y_copy(3, 1).wait_recv()
    x_start(3, 0)
    y_copy(1, 0).wait_recv()
    x_start(1, 1)

    for i, j in ((0, 3), (1, 1), (1, 2), (1, 3), (2, 3)):
        basis_block(i, j)
    known = basis_sums()

    y_copy(2, 0).wait_recv()
    x_start(2, 1)
    y_copy(2, 1).wait_recv()
    x_start(2, 0)

    x_wait(3)
    x_wait(1)
    chain(3, 1)
    combine(3, 1)
    x_wait(2)
    chain(2)
    combine(2)

    krylov_copy = pltpu.make_async_copy(w, krylov, out_sem.at[0])
    krylov_copy.start()

    fresh = {}
    for first in (0, 2):
        new = range(first, first + 2)
        pairs = [(b, k) for k in new for b in range(NB)]
        pairs += [(NB + t, k) for k in new for t in range(k + 1)]
        left = {b: (bas, b) for b in range(NB)}
        left.update({NB + t: (w, t) for t in range(first + 2)})
        totals = products(left, {k: (w, k) for k in new}, pairs)
        for t, k in pairs:
            if t >= NB:
                totals[NB + k, t - NB] = totals[t, k]
        fresh.update(totals)
        for k in new:
            for i in range(2):
                sums[NB + k, pl.ds(8 * i, 8)] = merge([fresh[b, k] for b in range(8 * i, 8 * i + 8)])
    for k in range(S):
        sums[NB + k, pl.ds(16, 8)] = merge([fresh[b, k] for b in range(16, 24)])
    total = []
    for i in range(3):
        fresh_part = merge_lanes({NB + k: sums[NB + k, pl.ds(8 * i, 8)] for k in range(S)})
        total.append(jnp.where(column_of < NB, known[i], fresh_part))
    packed = jnp.where(lane < 32, total[0], jnp.where(lane < 64, total[1], total[2]))

    def exchange(phase, value):
        me = mine[phase]
        slots[phase, me] = value

        def copy(to, spot):
            return pltpu.make_async_remote_copy(
                slots.at[phase, me],
                slots.at[phase, spot],
                as_.at[phase, to],
                ar.at[phase, spot],
                device_id=group_peer(phase, to),
                device_id_type=MESH,
            )

        def send(i, carry):
            copy((me + i) % 16, me).start()
            return carry

        def receive(i, carry):
            other = (me + i) % 16
            copy(other, other).wait_recv()
            return carry

        lax.fori_loop(1, 16, send, 0)
        lax.fori_loop(1, 16, receive, 0)
        total = slots[phase, 0]
        for m in range(1, 16):
            total = total + slots[phase, m]

        def sent(i, carry):
            copy((me + i) % 16, me).wait_send()
            return carry

        return total, lambda: lax.fori_loop(1, 16, sent, 0)

    packed, drain0 = exchange(0, packed)
    packed, drain1 = exchange(1, packed)

    products_out[...] = packed

    drain0()
    drain1()
    for d in range(4):
        for h in range(2):
            if d > 0:
                y_copy(d, h).wait_send()

            @pl.when(sends[h])
            def _():
                x_copy(d, h).wait_send()

    for side in range(2):

        @pl.when(sends[side])
        def _():
            for copy in side_copies(side):
                copy.wait_send()
    krylov_copy.wait()


def normalize(packed_ref, krylov, basis, block, proj, factor, w, bas, cf, in_sem, out_sem):
    def arrive(v):
        return (
            pltpu.make_async_copy(basis.at[:, v], bas.at[:, v], in_sem.at[0, v]),
            pltpu.make_async_copy(krylov.at[:, v], w.at[:, v], in_sem.at[1, v]),
        )

    def leave(v):
        return pltpu.make_async_copy(w.at[:, v], block.at[:, v], out_sem.at[v])

    for v in range(VARS):
        for copy in arrive(v):
            copy.start()

    sub = lax.broadcasted_iota(jnp.int32, (8, 128), 0)
    lane = lax.broadcasted_iota(jnp.int32, (8, 128), 1)
    wide_row = lax.broadcasted_iota(jnp.int32, (NZ, 128), 0)
    wide_lane = lax.broadcasted_iota(jnp.int32, (NZ, 128), 1)
    packed = packed_ref[...] / TOTAL
    means = jnp.concatenate([packed, pltpu.roll(packed, 96, 1), pltpu.roll(packed, 64, 1)], axis=0)
    column = pltpu.roll(means, 128 - NB, 1)
    proj[...] = jnp.concatenate([column, jnp.zeros((128 - NZ, 128), F32)], axis=0).T[0:S, 0:NB]
    coefs = jnp.where(jnp.logical_and(wide_row < NB, wide_lane < S), column, 0.0)
    half = jnp.where(jnp.logical_and(wide_row < NB, wide_lane < NB), means, 0.0)
    rest = -coefs
    for b in range(NB):
        rest = rest + half[:, b : b + 1] * coefs[b : b + 1]
    cross = [jnp.sum(coefs[:, s : s + 1] * rest, axis=0, keepdims=True) for s in range(S)]
    gram = [[None] * S for _ in range(S)]
    for s in range(S):
        for t in range(s + 1):
            value = column[NB + s : NB + s + 1, t : t + 1] + cross[s][:, t : t + 1] + cross[t][:, s : s + 1]
            gram[s][t] = jnp.broadcast_to(value, (8, 128))

    lower = [[None] * S for _ in range(S)]
    inverse = [[None] * S for _ in range(S)]
    for j in range(S):
        value = gram[j][j]
        for k in range(j):
            value = value - lower[j][k] * lower[j][k]
        lower[j][j] = jnp.sqrt(value)
        inverse[j][j] = 1.0 / lower[j][j]
        for i in range(j + 1, S):
            value = gram[i][j]
            for k in range(j):
                value = value - lower[i][k] * lower[j][k]
            lower[i][j] = value * inverse[j][j]
    for j in range(S):
        for i in range(j + 1, S):
            value = lower[i][j] * inverse[j][j]
            for k in range(j + 1, i):
                value = value + lower[i][k] * inverse[k][j]
            inverse[i][j] = -inverse[i][i] * value
    upper_factor = jnp.zeros((8, 128), F32)
    for s in range(S):
        for t in range(s + 1):
            upper_factor = jnp.where(jnp.logical_and(sub == t, lane == s), lower[s][t], upper_factor)
    factor[...] = upper_factor[0:S, 0:S]

    for s in range(S):
        value = None
        for t in range(s + 1):
            term = jnp.broadcast_to(coefs[:, t : t + 1], (NZ, 128)) * inverse[s][t][0:1]
            value = term if value is None else value + term
        cf[s] = -value
        for t in range(s + 1):
            cf[s, NB + t : NB + t + 1] = inverse[s][t][0:1]

    def finish(v, carry):
        for copy in arrive(v):
            copy.wait()

        def weight(s, n):
            return jnp.broadcast_to(cf[s, n : n + 1], (8, 128))

        totals = [[None] * LAYERS for _ in range(S)]
        for n in range(NZ):
            vectors = [(w[n - NB, v, l] if n >= NB else bas[n, v, l]) for l in range(LAYERS)]
            for s in range(S):
                if n >= NB and n - NB > s:
                    continue
                m = weight(s, n)
                for l in range(LAYERS):
                    term = m * vectors[l]
                    totals[s][l] = term if totals[s][l] is None else totals[s][l] + term
        for s in range(S):
            for l in range(LAYERS):
                w[s, v, l] = totals[s][l]
        leave(v).start()
        return carry

    lax.fori_loop(0, VARS, finish, 0)

    for v in range(VARS):
        leave(v).wait()


def shards(start, shifted_diag, face_coef, mixing, neighbours, basis):
    view = start.reshape(4, VARS, LAYERS, 2, 128).transpose(1, 2, 3, 0, 4).reshape(VARS, LAYERS, 8, 128)
    vectors = basis.reshape(NB, 4, VARS, LAYERS, 2, 128).transpose(0, 2, 3, 4, 1, 5)
    vectors = vectors.reshape(NB, VARS, LAYERS, 8, 128)
    hbm = pl.BlockSpec(memory_space=pltpu.HBM)
    vmem = pl.BlockSpec(memory_space=pltpu.VMEM)
    dma = pltpu.SemaphoreType.DMA
    krylov, packed = pl.pallas_call(
        kernel,
        out_shape=(
            jax.ShapeDtypeStruct((S, VARS, LAYERS, 8, 128), F32),
            jax.ShapeDtypeStruct((8, 128), F32),
        ),
        in_specs=[hbm] * 7,
        out_specs=(hbm, vmem),
        scratch_shapes=[
            pltpu.VMEM((4, 4, VARS, WIDE, 8, 128), F32),
            pltpu.VMEM((VARS, WIDE, 8, 128), F32),
            pltpu.VMEM((S, VARS, LAYERS, 8, 128), F32),
            pltpu.VMEM((NB, VARS, LAYERS, 8, 128), F32),
            pltpu.VMEM((FACES, LAYERS * FACE), F32),
            pltpu.VMEM((FACES, LAYERS * FACE), jnp.int32),
            pltpu.VMEM((16, 128), F32),
            pltpu.VMEM((2, FACES, 3 * FACE), F32),
            pltpu.VMEM((2, FACES, 3 * FACE), jnp.int32),
            pltpu.VMEM((2, 16, 128), F32),
            pltpu.VMEM((VARS, VARS), F32),
            pltpu.VMEM((4, 8 * S, 24 * S), F32),
            pltpu.VMEM((4, WIDE, 8, 128), F32),
            pltpu.VMEM((WIDE, 2, FACE, FACE), BF16),
            pltpu.VMEM((VARS * VARS, 8, 128), F32),
            pltpu.VMEM((NZ, NZ, 128), F32),
            pltpu.VMEM((2, 16, 8, 128), F32),
            dma((7,)),
            dma((4, 2)),
            dma((4, 2)),
            dma((4, 2)),
            dma((4, 2)),
            dma((2, 3)),
            dma((2, 3)),
            dma((2, 16)),
            dma((2, 16)),
            dma((1,)),
        ],
        compiler_params=pltpu.CompilerParams(
            collective_id=0, has_side_effects=True, vmem_limit_bytes=56 * 1024 * 1024
        ),
        name="krylov_block",
    )(view, face_coef, neighbours, shifted_diag.reshape(16, 128), vectors, mixing, jnp.asarray(time_tables()))
    block, proj, factor = pl.pallas_call(
        normalize,
        out_shape=(
            jax.ShapeDtypeStruct((S, VARS, LAYERS, 8, 128), F32),
            jax.ShapeDtypeStruct((S, NB), F32),
            jax.ShapeDtypeStruct((S, S), F32),
        ),
        in_specs=[vmem, hbm, hbm],
        out_specs=(hbm, vmem, vmem),
        scratch_shapes=[
            pltpu.VMEM((S, VARS, LAYERS, 8, 128), F32),
            pltpu.VMEM((NB, VARS, LAYERS, 8, 128), F32),
            pltpu.VMEM((S, NZ, 128), F32),
            dma((2, VARS)),
            dma((VARS,)),
        ],
        compiler_params=pltpu.CompilerParams(vmem_limit_bytes=56 * 1024 * 1024),
        name="normalize",
    )(packed, krylov, vectors)
    block = block.reshape(S, VARS, LAYERS, 2, 4, 128).transpose(0, 4, 1, 2, 3, 5)
    return block.reshape(S, 4, VARS, LAYERS * FACE), proj.T, factor


def solution(mesh):
    return jax.shard_map(
        shards,
        mesh=mesh,
        in_specs=(
            P("inst", None, "space"),
            P("space"),
            P(None, "space"),
            P(),
            P(None, "space"),
            P(None, "inst", None, "space"),
        ),
        out_specs=(P(None, "inst", None, "space"), P(), P()),
        check_vma=False,
    )
```

time: 95.1 us -> 49.8 us (0.52)
  Pallas kernels: 84.8 us -> 49 us
  local copies, waits for them, and re-layouts: 9.29 us -> 0 us
    pallas_call x1, Pallas kernels: 84.8 us -> 44 us  [shards(): pl.pallas_call(kernel, out_shape=(jax.ShapeDtypeStruct((S, VARS, LAYERS,...]
    unnamed x17 -> x0, local copies, waits for them, and re-layouts: 9.29 us -> none
    pallas_call x0 -> x1, Pallas kernels: none -> 5.01 us  [shards(): pl.pallas_call(normalize, out_shape=(jax.ShapeDtypeStruct((S, VARS, LAYER...]
where the time goes in v2:
time: 49.8 us; the launch traced here: 49.6 us
  Pallas kernels  49 us (98%)
  between operations  0.64 us (1%)
    pallas_call x1, Pallas kernels, shards(): pl.pallas_call(kernel, out_shape=(jax.ShapeDtypeStruct((S, VARS, LAYERS,...  44 us
    pallas_call x1, Pallas kernels, shards(): pl.pallas_call(normalize, out_shape=(jax.ShapeDtypeStruct((S, VARS, LAYER...  5.01 us

profile of v2, /device:TPU:1, one launch (start us, length us, event | category | flops | bytes accessed | tf_op | source)
XLA Modules:
  0.0 49.6 jit_solution(10287223089978359563)
XLA Ops:
  0.6 44.0 %krylov_block.1 = (f32[4,7,8,8,128]{4,3,2,1,0:T(8,128)}, f32[8,128]{1,0:T(8,128)}) custom-call(f32[7,8,8,128]{3,2,1,0:T(8,128)} %bitcast.19, f32[6,2048]{1,0:T(8,128)} %coef.1, s32[6,2048]{1,0:T(8,128)} %near.1, f32[16,128]{1,0:T(8,128)} %bitcast.20, f32[20,7,8,8,128]{4,3,2,1,0:T(8,128)} %bitcast.17, f32[7,7]{1,0:T(8,128)} %mixing.1, ...), custom_call_target="tpu_custom_call" | custom-call | tf_op jit(solution)/shard_map/krylov_block/pallas_call | solution.py:615
  44.6 5.0 %normalize.1 = (f32[4,7,8,8,128]{4,3,2,1,0:T(8,128)}, f32[4,20]{1,0:T(4,128)}, f32[4,4]{1,0:T(4,128)}) custom-call(f32[8,128]{1,0:T(8,128)} %get-tuple-element.8.packed_ref, f32[4,7,8,8,128]{4,3,2,1,0:T(8,128)} %get-tuple-element.9.krylov, f32[20,7,8,8,128]{4,3,2,1,0:T(8,128)} %bitcast.18), custom_call_target="tpu_custom_call" | custom-call | tf_op jit(solution)/shard_map/normalize/pallas_call | solution.py:657

commit v3 on v2

--- a/solution.py
+++ b/solution.py
@@ -20,8 +20,16 @@
 MESH = pl.DeviceIdType.MESH
 F32 = jnp.float32
 BF16 = jnp.bfloat16
-UNITS = 14
 TOTAL = float(NT * VARS * 131072)
+
+
+GATHER = lax.GatherDimensionNumbers(
+    offset_dims=(),
+    collapsed_slice_dims=(1,),
+    start_index_map=(1,),
+    operand_batching_dims=(0,),
+    start_indices_batching_dims=(0,),
+)
 
 
 def time_tables():
@@ -43,24 +51,53 @@
     return np.concatenate([high, high, low], axis=2).astype(np.float32)
 
 
+def basis_parts():
+    blocks = {}
+    for a in range(NB):
+        for b in range(a, NB):
+            blocks.setdefault((a // 8, b // 5), []).append((a, b))
+    blocks[1, 1] += blocks.pop((2, 3))
+    parts, at = [], 0
+    for pairs in blocks.values():
+        parts.append((pairs, at))
+        at += -(-len(pairs) // 16)
+    return parts
+
+
+PARTS = basis_parts()
+
+
+def pair_table():
+    table = np.zeros((2, 256), np.int32)
+    for pairs, at in PARTS:
+        for i, pair in enumerate(pairs):
+            table[:, 16 * at + i] = pair
+    return table.reshape(4, 128)
+
+
+def take(x, index):
+    return lax.gather(
+        x, index[:, :, None], GATHER, slice_sizes=(1, 1), mode=lax.GatherScatterMode.PROMISE_IN_BOUNDS
+    )
+
+
 def kernel(
     start, coef, near, diag, basis, mixing, times,
     krylov, products_out,
     u, u4, w, bas, coef_own, near_own, diag_own, coef_side, near_side, diag_side,
-    mixing_own, tables, geo, weights, mix, sums, slots,
-    load_sem, ys, yr, xs, xr, gs, gr, as_, ar, out_sem,
+    mixing_own, tables, geo, weights, mix, sums, slots, planes,
+    load_sem, ys, yr, xs, xr, gs, gr, sum_sem, out_sem,
 ):
     p, q = lax.axis_index("space"), lax.axis_index("inst")
     z, x, c = p // 8, (p // 2) % 4, p % 2
     has_low, has_high = p > 0, p < 63
     y_up, y_down = (q + 1) % 4, (q + 3) % 4
 
-    def group_peer(phase, m):
-        if phase == 0:
-            return {"space": (z * 4 + m // 4) * 2 + c, "inst": m % 4}
-        return {"space": ((m // 2) * 4 + x) * 2 + m % 2, "inst": q}
-
-    mine = (x * 4 + q, z * 2 + c)
+    def chip(dz, dx, dy, core):
+        return {"space": ((z + dz) % 8 * 4 + (x + dx) % 4) * 2 + core, "inst": (q + dy) % 4}
+
+    plane = [(0, dx, dy) for dx in range(4) for dy in range(4)]
+    column = [(dz, 0, 0) for dz in range(8)]
 
     loads = [
         pltpu.make_async_copy(coef, coef_own, load_sem.at[0]),
@@ -76,27 +113,32 @@
 
     barrier = pltpu.get_barrier_semaphore()
 
-    def greet(phase):
-        def body(i, carry):
-            pl.semaphore_signal(
-                barrier, inc=1, device_id=group_peer(phase, (mine[phase] + i) % 16), device_id_type=MESH
-            )
-            return carry
-
-        lax.fori_loop(1, 16, body, 0)
-
-    greet(0)
-    greet(1)
-
-    @pl.when(has_low)
+    def greet(to):
+        pl.semaphore_signal(barrier, inc=1, device_id=to, device_id_type=MESH)
+
+    @pl.when(c == 0)
     def _():
-        pl.semaphore_signal(barrier, inc=1, device_id={"space": p - 1, "inst": q}, device_id_type=MESH)
-
-    @pl.when(has_high)
+        for at in column[1:]:
+            greet(chip(*at, 0))
+        for at in plane[1:]:
+            greet(chip(*at, 0))
+        for at in plane:
+            greet(chip(*at, 1))
+
+        @pl.when(jnp.logical_and(x == 0, z > 0))
+        def _():
+            greet({"space": p - 1, "inst": q})
+
+    @pl.when(c == 1)
     def _():
-        pl.semaphore_signal(barrier, inc=1, device_id={"space": p + 1, "inst": q}, device_id_type=MESH)
-
-    pl.semaphore_wait(barrier, 30 + jnp.where(has_low, 1, 0) + jnp.where(has_high, 1, 0))
+        for at in column:
+            greet(chip(*at, 0))
+        greet({"space": p, "inst": y_up})
+        greet({"space": p, "inst": y_down})
+
+        @pl.when(has_high)
+        def _():
+            greet({"space": p + 1, "inst": q})
 
     def y_copy(d, h):
         dst = u.at[0, d, :, pl.ds(4 + 4 * h, 4)]
@@ -147,30 +189,6 @@
         def _():
             x_copy(d, side).start()
 
-    y_copy(3, 0).start()
-    y_copy(1, 1).start()
-    for side in range(2):
-
-        @pl.when(sends[side])
-        def _():
-            for copy in side_copies(side):
-                copy.start()
-
-        x_start(0, side)
-    y_copy(3, 1).start()
-    y_copy(1, 0).start()
-
-    for side in range(2):
-
-        @pl.when(jnp.logical_not(hears[side]))
-        def _():
-            coef_side[side] = jnp.zeros((FACES, 3 * FACE), F32)
-            near_side[side] = jnp.zeros((FACES, 3 * FACE), jnp.int32)
-            diag_side[side] = jnp.zeros((16, 128), F32)
-            for d in range(4):
-                first = 0 if side == 0 else 12
-                u[0, d, :, pl.ds(first, 4)] = jnp.zeros((VARS, 4, 8, 128), F32)
-
     sub = lax.broadcasted_iota(jnp.int32, (8, 128), 0)
     lane = lax.broadcasted_iota(jnp.int32, (8, 128), 1)
     upper = sub >= 4
@@ -214,18 +232,6 @@
     coefs, nears, diags = coef_own[...], near_own[...], diag_own[...]
     for layer in range(LAYERS):
         place(4 + layer, coefs, nears, layer * FACE, diags[2 * layer : 2 * layer + 2])
-    for side in range(2):
-
-        @pl.when(hears[side])
-        def _():
-            for copy in side_copies(side):
-                copy.wait_recv()
-
-        coefs, nears, diags = coef_side[side], near_side[side], diag_side[side]
-        for layer in range(3):
-            first = 10 + 2 * layer if side == 0 else 2 * layer
-            place((1 if side == 0 else 12) + layer, coefs, nears, layer * FACE, diags[first : first + 2])
-
     def within(groups, layer):
         rows = []
         for values in groups:
@@ -254,41 +260,36 @@
             results.append(result)
         return results
 
-    def step(pairs, low, high):
-        count = max(n for n in range(1, UNITS // len(pairs) + 1) if (high - low) % n == 0)
-
-        def body(i, carry):
-            layers = [low + count * i + e for e in range(count)]
-            fluxes = []
-            for b in layers:
-                centers = [[src[v, b] for v in range(VARS)] for src, _ in pairs]
-                inner = within(centers, b)
-                g = [geo[f, b] for f in range(3)]
-                for (src, _), center, inside in zip(pairs, centers, inner):
-                    fluxes.append(
-                        [
-                            g[0] * center[v] - g[1] * src[v, b - 1] - g[2] * src[v, b + 1] - inside[v]
-                            for v in range(VARS)
-                        ]
-                    )
-            units = [(src, dst, b) for b in layers for src, dst in pairs]
-            for i in range(VARS):
-                totals = [geo[3, b] * src[i, b] for src, _, b in units]
-                for j in range(VARS):
-                    m = mix[i * VARS + j]
-                    totals = [t + m * flux[j] for t, flux in zip(totals, fluxes)]
-                for (_, dst, b), total in zip(units, totals):
-                    dst[i, b] = total
-            return carry
-
-        lax.fori_loop(0, (high - low) // count, body, 0)
-
-    def chain(*groups):
-        low = 1 if groups[0] == 0 else 2
+    def step(groups, j, layers):
+        pairs = [(u.at[j, d], u4 if j == 3 else u.at[j + 1, d]) for d in groups]
+        fluxes = []
+        for b in layers:
+            centers = [[src[v, b] for v in range(VARS)] for src, _ in pairs]
+            inner = within(centers, b)
+            g = [geo[f, b] for f in range(3)]
+            for (src, _), center, inside in zip(pairs, centers, inner):
+                fluxes.append(
+                    [
+                        g[0] * center[v] - g[1] * src[v, b - 1] - g[2] * src[v, b + 1] - inside[v]
+                        for v in range(VARS)
+                    ]
+                )
+        units = [(src, dst, b) for b in layers for src, dst in pairs]
+        for i in range(VARS):
+            totals = [geo[3, b] * src[i, b] for src, _, b in units]
+            for n in range(VARS):
+                m = mix[i * VARS + n]
+                totals = [t + m * flux[n] for t, flux in zip(totals, fluxes)]
+            for (_, dst, b), total in zip(units, totals):
+                dst[i, b] = total
+
+    def inside(*groups):
         for j in range(3):
-            step([(u.at[j, d], u.at[j + 1, d]) for d in groups], low + j, 16 - low - j)
-        if groups[0] == 0:
-            step([(u.at[3, 0], u4)], 4, 12)
+            step(groups, j, range(5 + j, 11 - j))
+
+    def outside(groups, j):
+        reach = (4 if groups[0] == 0 else 3) - j
+        step(groups, j, [*range(5 - reach, 5 + j), *range(11 - j, 11 + reach)])
 
     def combine(*groups):
         table = jnp.concatenate([tables[d] for d in groups], axis=1).astype(BF16)
@@ -312,16 +313,32 @@
                     else:
                         w[k, v, l] += term
 
-    bits = {k: (sub // k) % 2 == 1 for k in (1, 2, 4)}
     zero = jnp.zeros((8, 128), F32)
 
-    def merge(parts):
-        for k in (1, 2, 4):
-            parts = [
-                jnp.where(bits[k], b, a) + pltpu.roll(jnp.where(bits[k], a, b), k, 0)
-                for a, b in zip(parts[::2], parts[1::2])
-            ]
+    def merge(parts, first=1, last=64):
+        k = first
+        while k <= last:
+            bit = (lane // k) % 2 == 1
+            merged = []
+            for a, b in zip(parts[::2], parts[1::2]):
+                if a is None and b is None:
+                    merged.append(None)
+                    continue
+                a, b = zero if a is None else a, zero if b is None else b
+                merged.append(jnp.where(bit, b, a) + pltpu.roll(jnp.where(bit, a, b), k, 1))
+            parts, k = merged, 2 * k
         return parts[0]
+
+    def sixteens(values, at):
+        for i in range(0, len(values), 16):
+            group = values[i : i + 16]
+            sums[at + i // 16] = merge(group + [None] * (16 - len(group)), last=8)
+
+    def row(at, count):
+        total = merge([sums[at + i] for i in range(count)] + [None] * (8 - count), first=16)
+        for k in (4, 2, 1):
+            total = total + pltpu.roll(total, k, 0)
+        return total
 
     def products(left, right, pairs):
         def body(v, totals):
@@ -335,46 +352,14 @@
         totals = lax.fori_loop(0, VARS, body, (zero,) * len(pairs))
         return dict(zip(pairs, totals))
 
-    def basis_block(i, j):
-        rows = range(8 * i, min(8 * i + 8, NB))
-        columns = range(5 * j, 5 * j + 5)
+    def basis_part(i):
+        pairs, at = PARTS[i]
         totals = products(
-            {a: (bas, a) for a in rows},
-            {b: (bas, b) for b in columns},
-            [(a, b) for a in rows for b in columns if a <= b],
-        )
-        for b in columns:
-            sums[b, pl.ds(8 * i, 8)] = merge([totals.get((a, b), zero) for a in range(8 * i, 8 * i + 8)])
-
-    wide_row = lax.broadcasted_iota(jnp.int32, (NZ, 128), 0)
-    wide_lane = lax.broadcasted_iota(jnp.int32, (NZ, 128), 1)
-
-    def merge_lanes(columns):
-        parts = [columns.get(i) for i in range(32)]
-        for k in (1, 2, 4, 8, 16):
-            bit = (lane // k) % 2 == 1
-            merged = []
-            for a, b in zip(parts[::2], parts[1::2]):
-                if a is None and b is None:
-                    merged.append(None)
-                    continue
-                a, b = zero if a is None else a, zero if b is None else b
-                merged.append(jnp.where(bit, b, a) + pltpu.roll(jnp.where(bit, a, b), k, 1))
-            parts = merged
-        total = parts[0]
-        total = total + pltpu.roll(total, 32, 1)
-        return total + pltpu.roll(total, 64, 1)
-
-    column_of = lane % 32
-
-    def basis_sums():
-        result = []
-        for i in range(3):
-            part = merge_lanes({b: sums[b, pl.ds(8 * i, 8)] for b in range(8 * i, NB)})
-            part = jnp.where(sub + 8 * i <= column_of, part, 0.0)
-            part = jnp.where(sub + 8 * i == column_of, 0.5 * part, part)
-            result.append(jnp.where(column_of < NB, part, 0.0))
-        return result
+            {a: (bas, a) for a, _ in pairs},
+            {b: (bas, b) for _, b in pairs},
+            pairs,
+        )
+        sixteens([(0.5 if a == b else 1.0) * totals[a, b] for a, b in pairs], at)
 
     def x_wait(d):
         for side in range(2):
@@ -383,11 +368,60 @@
             def _():
                 x_copy(d, side).wait_recv()
 
+    loads[6].wait()
+    for i in range(2):
+        basis_part(i)
+
+    @pl.when(c == 0)
+    def _():
+        pl.semaphore_wait(barrier, 30 + jnp.where(has_low, 1, 0))
+
+    @pl.when(c == 1)
+    def _():
+        pl.semaphore_wait(barrier, 18 + jnp.where(jnp.logical_and(x == 3, z < 7), 1, 0))
+
+    y_copy(3, 0).start()
+    y_copy(1, 1).start()
+    for side in range(2):
+
+        @pl.when(sends[side])
+        def _():
+            for copy in side_copies(side):
+                copy.start()
+
+        x_start(0, side)
+    y_copy(3, 1).start()
+    y_copy(1, 0).start()
+
+    for side in range(2):
+
+        @pl.when(jnp.logical_not(hears[side]))
+        def _():
+            coef_side[side] = jnp.zeros((FACES, 3 * FACE), F32)
+            near_side[side] = jnp.zeros((FACES, 3 * FACE), jnp.int32)
+            diag_side[side] = jnp.zeros((16, 128), F32)
+            for d in range(4):
+                first = 0 if side == 0 else 12
+                u[0, d, :, pl.ds(first, 4)] = jnp.zeros((VARS, 4, 8, 128), F32)
+
+    for i in range(2, len(PARTS)):
+        basis_part(i)
+    known = (row(0, 8), row(8, 8))
     loads[4].wait()
     loads[5].wait()
-    x_wait(0)
-    chain(0)
-    combine(0)
+    inside(0)
+
+    for side in range(2):
+
+        @pl.when(hears[side])
+        def _():
+            for copy in side_copies(side):
+                copy.wait_recv()
+
+        coefs, nears, diags = coef_side[side], near_side[side], diag_side[side]
+        for layer in range(3):
+            first = 10 + 2 * layer if side == 0 else 2 * layer
+            place((1 if side == 0 else 12) + layer, coefs, nears, layer * FACE, diags[first : first + 2])
 
     y_copy(3, 0).wait_recv()
     y_copy(2, 0).start()
@@ -396,36 +430,39 @@
     x_start(3, 1)
     x_start(1, 0)
 
-    loads[6].wait()
-    for i, j in ((0, 0), (0, 1), (0, 2)):
-        basis_block(i, j)
+    x_wait(0)
+    outside((0,), 0)
+    outside((0,), 1)
 
     y_copy(3, 1).wait_recv()
     x_start(3, 0)
     y_copy(1, 0).wait_recv()
     x_start(1, 1)
 
-    for i, j in ((0, 3), (1, 1), (1, 2), (1, 3), (2, 3)):
-        basis_block(i, j)
-    known = basis_sums()
+    outside((0,), 2)
+    step((0,), 3, range(4, 12))
+    combine(0)
 
     y_copy(2, 0).wait_recv()
     x_start(2, 1)
     y_copy(2, 1).wait_recv()
     x_start(2, 0)
 
+    inside(3, 1)
+    inside(2)
+
     x_wait(3)
     x_wait(1)
-    chain(3, 1)
+    for j in range(3):
+        outside((3, 1), j)
     combine(3, 1)
     x_wait(2)
-    chain(2)
+    for j in range(3):
+        outside((2,), j)
     combine(2)
-
     krylov_copy = pltpu.make_async_copy(w, krylov, out_sem.at[0])
     krylov_copy.start()
 
-    fresh = {}
     for first in (0, 2):
         new = range(first, first + 2)
         pairs = [(b, k) for k in new for b in range(NB)]
@@ -433,63 +470,71 @@
         left = {b: (bas, b) for b in range(NB)}
         left.update({NB + t: (w, t) for t in range(first + 2)})
         totals = products(left, {k: (w, k) for k in new}, pairs)
-        for t, k in pairs:
-            if t >= NB:
-                totals[NB + k, t - NB] = totals[t, k]
-        fresh.update(totals)
-        for k in new:
-            for i in range(2):
-                sums[NB + k, pl.ds(8 * i, 8)] = merge([fresh[b, k] for b in range(8 * i, 8 * i + 8)])
-    for k in range(S):
-        sums[NB + k, pl.ds(16, 8)] = merge([fresh[b, k] for b in range(16, 24)])
-    total = []
-    for i in range(3):
-        fresh_part = merge_lanes({NB + k: sums[NB + k, pl.ds(8 * i, 8)] for k in range(S)})
-        total.append(jnp.where(column_of < NB, known[i], fresh_part))
-    packed = jnp.where(lane < 32, total[0], jnp.where(lane < 64, total[1], total[2]))
-
-    def exchange(phase, value):
-        me = mine[phase]
-        slots[phase, me] = value
-
-        def copy(to, spot):
-            return pltpu.make_async_remote_copy(
-                slots.at[phase, me],
-                slots.at[phase, spot],
-                as_.at[phase, to],
-                ar.at[phase, spot],
-                device_id=group_peer(phase, to),
-                device_id_type=MESH,
-            )
-
-        def send(i, carry):
-            copy((me + i) % 16, me).start()
-            return carry
-
-        def receive(i, carry):
-            other = (me + i) % 16
-            copy(other, other).wait_recv()
-            return carry
-
-        lax.fori_loop(1, 16, send, 0)
-        lax.fori_loop(1, 16, receive, 0)
-        total = slots[phase, 0]
-        for m in range(1, 16):
-            total = total + slots[phase, m]
-
-        def sent(i, carry):
-            copy((me + i) % 16, me).wait_send()
-            return carry
-
-        return total, lambda: lax.fori_loop(1, 16, sent, 0)
-
-    packed, drain0 = exchange(0, packed)
-    packed, drain1 = exchange(1, packed)
-
+        sixteens([totals.get((b, k)) for k in new for b in range(NZ)], 16 + 3 * (first // 2))
+    packed = jnp.where(sub == 0, row(16, 6), jnp.where(sub == 1, known[0], known[1]))[0:4]
+
+    def plane_copy(at, spot):
+        return pltpu.make_async_remote_copy(
+            slots.at[spot], slots.at[spot], sum_sem.at[0], sum_sem.at[1], device_id=chip(*at, 0), device_id_type=MESH
+        )
+
+    def plane_all(count):
+        some = slots.at[pl.ds(0, count)]
+        return pltpu.make_async_remote_copy(
+            some, some, sum_sem.at[0], sum_sem.at[1], device_id=chip(0, 0, 1, 0), device_id_type=MESH
+        )
+
+    def column_copy(at, core):
+        return pltpu.make_async_remote_copy(
+            planes.at[z], planes.at[z], sum_sem.at[2], sum_sem.at[3], device_id=chip(*at, core), device_id_type=MESH
+        )
+
+    def column_all(ref, count):
+        some = ref.at[pl.ds(0, count)]
+        return pltpu.make_async_remote_copy(
+            some, some, sum_sem.at[2], sum_sem.at[3], device_id=chip(0, 0, 1, 0), device_id_type=MESH
+        )
+
+    def add_up(ref, count):
+        parts = [ref[i] for i in range(count)]
+        while len(parts) > 1:
+            parts = [a + b for a, b in zip(parts[::2], parts[1::2])]
+        return parts[0]
+
+    spot = 16 * c + x * 4 + q
+    slots[spot] = packed
+    far = sorted(plane, key=lambda at: -sum(min(d, 4 - d) for d in at))
+
+    @pl.when(c == 1)
+    def _():
+        for at in far:
+            plane_copy(at, spot).start()
+        column_all(planes, 8).wait_recv()
+
+    @pl.when(c == 0)
+    def _():
+        for at in far[:-1]:
+            plane_copy(at, spot).start()
+        plane_all(31).wait_recv()
+        planes[z] = add_up(slots, 32)
+        for dz in (4, 3, 5, 2, 6, 1, 7):
+            column_copy((dz, 0, 0), 1).start()
+            column_copy((dz, 0, 0), 0).start()
+        column_copy((0, 0, 0), 1).start()
+        column_all(planes, 7).wait_recv()
+
+    packed = add_up(planes, 8)
     products_out[...] = packed
 
-    drain0()
-    drain1()
+    @pl.when(c == 0)
+    def _():
+        plane_all(15).wait_send()
+        column_all(slots, 15).wait_send()
+
+    @pl.when(c == 1)
+    def _():
+        plane_all(16).wait_send()
+
     for d in range(4):
         for h in range(2):
             if d > 0:
@@ -508,7 +553,7 @@
     krylov_copy.wait()
 
 
-def normalize(packed_ref, krylov, basis, block, proj, factor, w, bas, cf, in_sem, out_sem):
+def normalize(packed_ref, pairs, krylov, basis, block, proj, factor, w, bas, cf, in_sem, out_sem):
     def arrive(v):
         return (
             pltpu.make_async_copy(basis.at[:, v], bas.at[:, v], in_sem.at[0, v]),
@@ -524,23 +569,26 @@
 
     sub = lax.broadcasted_iota(jnp.int32, (8, 128), 0)
     lane = lax.broadcasted_iota(jnp.int32, (8, 128), 1)
-    wide_row = lax.broadcasted_iota(jnp.int32, (NZ, 128), 0)
-    wide_lane = lax.broadcasted_iota(jnp.int32, (NZ, 128), 1)
     packed = packed_ref[...] / TOTAL
-    means = jnp.concatenate([packed, pltpu.roll(packed, 96, 1), pltpu.roll(packed, 64, 1)], axis=0)
-    column = pltpu.roll(means, 128 - NB, 1)
-    proj[...] = jnp.concatenate([column, jnp.zeros((128 - NZ, 128), F32)], axis=0).T[0:S, 0:NB]
-    coefs = jnp.where(jnp.logical_and(wide_row < NB, wide_lane < S), column, 0.0)
-    half = jnp.where(jnp.logical_and(wide_row < NB, wide_lane < NB), means, 0.0)
-    rest = -coefs
-    for b in range(NB):
-        rest = rest + half[:, b : b + 1] * coefs[b : b + 1]
-    cross = [jnp.sum(coefs[:, s : s + 1] * rest, axis=0, keepdims=True) for s in range(S)]
-    gram = [[None] * S for _ in range(S)]
-    for s in range(S):
-        for t in range(s + 1):
-            value = column[NB + s : NB + s + 1, t : t + 1] + cross[s][:, t : t + 1] + cross[t][:, s : s + 1]
-            gram[s][t] = jnp.broadcast_to(value, (8, 128))
+
+    def lanes(index):
+        return take(jnp.broadcast_to(packed[0:1], index.shape), index)
+
+    proj[...] = lanes(jnp.where(lane < NB, NZ * (sub % 4) + lane, 0))[0:S, 0:NB]
+
+    s_row = lax.broadcasted_iota(jnp.int32, (16, 128), 0) // 4
+    t_row = lax.broadcasted_iota(jnp.int32, (16, 128), 0) % 4
+    lane16 = lax.broadcasted_iota(jnp.int32, (16, 128), 1)
+    place = jnp.where(lane16 < NB, lane16, 0)
+    terms = jnp.where(lane16 < NB, -2.0 * lanes(place + NZ * s_row) * lanes(place + NZ * t_row), 0.0)
+    for i in range(2):
+        a = jnp.broadcast_to(pairs[i : i + 1, :], (16, 128))
+        b = jnp.broadcast_to(pairs[2 + i : 3 + i, :], (16, 128))
+        both = lanes(a + NZ * s_row) * lanes(b + NZ * t_row) + lanes(a + NZ * t_row) * lanes(b + NZ * s_row)
+        terms = terms + packed[1 + i : 2 + i] * both
+    whole = jnp.sum(terms, axis=1, keepdims=True)
+    whole = whole + lanes(NZ * jnp.maximum(s_row, t_row) + NB + jnp.minimum(s_row, t_row))
+    gram = [[jnp.broadcast_to(whole[4 * s + t : 4 * s + t + 1], (8, 128)) for t in range(S)] for s in range(S)]
 
     lower = [[None] * S for _ in range(S)]
     inverse = [[None] * S for _ in range(S)]
@@ -567,10 +615,13 @@
             upper_factor = jnp.where(jnp.logical_and(sub == t, lane == s), lower[s][t], upper_factor)
     factor[...] = upper_factor[0:S, 0:S]
 
+    row24 = lax.broadcasted_iota(jnp.int32, (NZ, 128), 0)
+    coefs = [lanes(row24 + NZ * k) for k in range(S)]
+
     for s in range(S):
         value = None
         for t in range(s + 1):
-            term = jnp.broadcast_to(coefs[:, t : t + 1], (NZ, 128)) * inverse[s][t][0:1]
+            term = coefs[t] * inverse[s][t][0:1]
             value = term if value is None else value + term
         cf[s] = -value
         for t in range(s + 1):
@@ -616,7 +667,7 @@
         kernel,
         out_shape=(
             jax.ShapeDtypeStruct((S, VARS, LAYERS, 8, 128), F32),
-            jax.ShapeDtypeStruct((8, 128), F32),
+            jax.ShapeDtypeStruct((4, 128), F32),
         ),
         in_specs=[hbm] * 7,
         out_specs=(hbm, vmem),
@@ -636,8 +687,9 @@
             pltpu.VMEM((4, WIDE, 8, 128), F32),
             pltpu.VMEM((WIDE, 2, FACE, FACE), BF16),
             pltpu.VMEM((VARS * VARS, 8, 128), F32),
-            pltpu.VMEM((NZ, NZ, 128), F32),
-            pltpu.VMEM((2, 16, 8, 128), F32),
+            pltpu.VMEM((22, 8, 128), F32),
+            pltpu.VMEM((32, 4, 128), F32),
+            pltpu.VMEM((8, 4, 128), F32),
             dma((7,)),
             dma((4, 2)),
             dma((4, 2)),
@@ -645,8 +697,7 @@
             dma((4, 2)),
             dma((2, 3)),
             dma((2, 3)),
-            dma((2, 16)),
-            dma((2, 16)),
+            dma((4,)),
             dma((1,)),
         ],
         compiler_params=pltpu.CompilerParams(
@@ -661,7 +712,7 @@
             jax.ShapeDtypeStruct((S, NB), F32),
             jax.ShapeDtypeStruct((S, S), F32),
         ),
-        in_specs=[vmem, hbm, hbm],
+        in_specs=[vmem, vmem, hbm, hbm],
         out_specs=(hbm, vmem, vmem),
         scratch_shapes=[
             pltpu.VMEM((S, VARS, LAYERS, 8, 128), F32),
@@ -672,7 +723,7 @@
         ],
         compiler_params=pltpu.CompilerParams(vmem_limit_bytes=56 * 1024 * 1024),
         name="normalize",
-    )(packed, krylov, vectors)
+    )(packed, jnp.asarray(pair_table()), krylov, vectors)
     block = block.reshape(S, VARS, LAYERS, 2, 4, 128).transpose(0, 4, 1, 2, 3, 5)
     return block.reshape(S, 4, VARS, LAYERS * FACE), proj.T, factor
 

time: 49.8 us -> 45.5 us (0.914)
  Pallas kernels: 49 us -> 44.8 us
    pallas_call x1, Pallas kernels: 44 us -> 39.8 us  [shards(): pl.pallas_call(kernel, out_shape=(jax.ShapeDtypeStruct((S, VARS, LAYERS,...]
where the time goes in v3:
time: 45.5 us; the launch traced here: 45.4 us
  Pallas kernels  44.8 us (98%)
  between operations  0.64 us (1%)
    pallas_call x1, Pallas kernels, shards(): pl.pallas_call(kernel, out_shape=(jax.ShapeDtypeStruct((S, VARS, LAYERS,...  39.8 us
    pallas_call x1, Pallas kernels, shards(): pl.pallas_call(normalize, out_shape=(jax.ShapeDtypeStruct((S, VARS, LAYER...  4.95 us

profile of v3, /device:TPU:1, one launch (start us, length us, event | category | flops | bytes accessed | tf_op | source)
XLA Modules:
  0.0 45.4 jit_solution(6195381888123349663)
XLA Ops:
  0.6 39.8 %krylov_block.1 = (f32[4,7,8,8,128]{4,3,2,1,0:T(8,128)}, f32[4,128]{1,0:T(4,128)}) custom-call(f32[7,8,8,128]{3,2,1,0:T(8,128)} %bitcast.19, f32[6,2048]{1,0:T(8,128)} %coef.1, s32[6,2048]{1,0:T(8,128)} %near.1, f32[16,128]{1,0:T(8,128)} %bitcast.20, f32[20,7,8,8,128]{4,3,2,1,0:T(8,128)} %bitcast.17, f32[7,7]{1,0:T(8,128)} %mixing.1, ...), custom_call_target="tpu_custom_call" | custom-call | tf_op jit(solution)/shard_map/krylov_block/pallas_call | solution.py:666
  40.5 4.9 %normalize.1 = (f32[4,7,8,8,128]{4,3,2,1,0:T(8,128)}, f32[4,20]{1,0:T(4,128)}, f32[4,4]{1,0:T(4,128)}) custom-call(f32[4,128]{1,0:T(4,128)} %get-tuple-element.8.packed_ref, s32[4,128]{1,0:T(4,128)} %constant.5.clone.pairs, f32[4,7,8,8,128]{4,3,2,1,0:T(8,128)} %get-tuple-element.9.krylov, f32[20,7,8,8,128]{4,3,2,1,0:T(8,128)} %bitcast.18), custom_call_target="tpu_custom_call" | custom-call | tf_op jit(solution)/shard_map/normalize/pallas_call | solution.py:708

commit v4 on v3

--- a/solution.py
+++ b/solution.py
@@ -67,11 +67,15 @@
 PARTS = basis_parts()
 
 
+def spot_of(b):
+    return b + 38 * (b >= 10)
+
+
 def pair_table():
     table = np.zeros((2, 256), np.int32)
     for pairs, at in PARTS:
         for i, pair in enumerate(pairs):
-            table[:, 16 * at + i] = pair
+            table[:, 16 * at + i] = [spot_of(b) for b in pair]
     return table.reshape(4, 128)
 
 
@@ -463,15 +467,16 @@
     krylov_copy = pltpu.make_async_copy(w, krylov, out_sem.at[0])
     krylov_copy.start()
 
-    for first in (0, 2):
-        new = range(first, first + 2)
-        pairs = [(b, k) for k in new for b in range(NB)]
-        pairs += [(NB + t, k) for k in new for t in range(k + 1)]
-        left = {b: (bas, b) for b in range(NB)}
-        left.update({NB + t: (w, t) for t in range(first + 2)})
-        totals = products(left, {k: (w, k) for k in new}, pairs)
-        sixteens([totals.get((b, k)) for k in new for b in range(NZ)], 16 + 3 * (first // 2))
-    packed = jnp.where(sub == 0, row(16, 6), jnp.where(sub == 1, known[0], known[1]))[0:4]
+    new = {k: (w, k) for k in range(S)}
+    for first in (0, 10):
+        some = range(first, first + 10)
+        pairs = [(b, k) for k in range(S) for b in some]
+        totals = products({b: (bas, b) for b in some}, new, pairs)
+        sixteens([totals[pair] for pair in pairs], 16 + 3 * (first // 10))
+    pairs = [(t, k) for k in range(S) for t in range(k + 1)]
+    totals = products(new, new, pairs)
+    sixteens([totals.get((t, k)) for k in range(S) for t in range(S)], 22)
+    packed = jnp.where(sub == 0, row(16, 7), jnp.where(sub == 1, known[0], known[1]))[0:4]
 
     def plane_copy(at, spot):
         return pltpu.make_async_remote_copy(
@@ -574,20 +579,23 @@
     def lanes(index):
         return take(jnp.broadcast_to(packed[0:1], index.shape), index)
 
-    proj[...] = lanes(jnp.where(lane < NB, NZ * (sub % 4) + lane, 0))[0:S, 0:NB]
+    def spots(b):
+        return b + jnp.where(b >= 10, 38, 0)
+
+    proj[...] = lanes(jnp.where(lane < NB, 10 * (sub % 4) + spots(lane), 0))[0:S, 0:NB]
 
     s_row = lax.broadcasted_iota(jnp.int32, (16, 128), 0) // 4
     t_row = lax.broadcasted_iota(jnp.int32, (16, 128), 0) % 4
     lane16 = lax.broadcasted_iota(jnp.int32, (16, 128), 1)
-    place = jnp.where(lane16 < NB, lane16, 0)
-    terms = jnp.where(lane16 < NB, -2.0 * lanes(place + NZ * s_row) * lanes(place + NZ * t_row), 0.0)
+    place = jnp.where(lane16 < NB, spots(lane16), 0)
+    terms = jnp.where(lane16 < NB, -2.0 * lanes(place + 10 * s_row) * lanes(place + 10 * t_row), 0.0)
     for i in range(2):
         a = jnp.broadcast_to(pairs[i : i + 1, :], (16, 128))
         b = jnp.broadcast_to(pairs[2 + i : 3 + i, :], (16, 128))
-        both = lanes(a + NZ * s_row) * lanes(b + NZ * t_row) + lanes(a + NZ * t_row) * lanes(b + NZ * s_row)
+        both = lanes(a + 10 * s_row) * lanes(b + 10 * t_row) + lanes(a + 10 * t_row) * lanes(b + 10 * s_row)
         terms = terms + packed[1 + i : 2 + i] * both
     whole = jnp.sum(terms, axis=1, keepdims=True)
-    whole = whole + lanes(NZ * jnp.maximum(s_row, t_row) + NB + jnp.minimum(s_row, t_row))
+    whole = whole + lanes(96 + 4 * jnp.maximum(s_row, t_row) + jnp.minimum(s_row, t_row))
     gram = [[jnp.broadcast_to(whole[4 * s + t : 4 * s + t + 1], (8, 128)) for t in range(S)] for s in range(S)]
 
     lower = [[None] * S for _ in range(S)]
@@ -616,7 +624,7 @@
     factor[...] = upper_factor[0:S, 0:S]
 
     row24 = lax.broadcasted_iota(jnp.int32, (NZ, 128), 0)
-    coefs = [lanes(row24 + NZ * k) for k in range(S)]
+    coefs = [lanes(jnp.where(row24 < NB, spots(row24), 0) + 10 * k) for k in range(S)]
 
     for s in range(S):
         value = None
@@ -687,7 +695,7 @@
             pltpu.VMEM((4, WIDE, 8, 128), F32),
             pltpu.VMEM((WIDE, 2, FACE, FACE), BF16),
             pltpu.VMEM((VARS * VARS, 8, 128), F32),
-            pltpu.VMEM((22, 8, 128), F32),
+            pltpu.VMEM((23, 8, 128), F32),
             pltpu.VMEM((32, 4, 128), F32),
             pltpu.VMEM((8, 4, 128), F32),
             dma((7,)),

time: 45.5 us -> 45.3 us (level)
  no operation moved by 1% of the time
where the time goes in v4:
time: 45.3 us; the launch traced here: 45.1 us
  Pallas kernels  44.5 us (98%)
  between operations  0.64 us (1%)
    pallas_call x1, Pallas kernels, shards(): pl.pallas_call(kernel, out_shape=(jax.ShapeDtypeStruct((S, VARS, LAYERS,...  39.5 us
    pallas_call x1, Pallas kernels, shards(): pl.pallas_call(normalize, out_shape=(jax.ShapeDtypeStruct((S, VARS, LAYER...  4.95 us

profile of v4, /device:TPU:1, one launch (start us, length us, event | category | flops | bytes accessed | tf_op | source)
XLA Modules:
  0.0 45.1 jit_solution(2748076515486220885)
XLA Ops:
  0.6 39.5 %krylov_block.1 = (f32[4,7,8,8,128]{4,3,2,1,0:T(8,128)}, f32[4,128]{1,0:T(4,128)}) custom-call(f32[7,8,8,128]{3,2,1,0:T(8,128)} %bitcast.19, f32[6,2048]{1,0:T(8,128)} %coef.1, s32[6,2048]{1,0:T(8,128)} %near.1, f32[16,128]{1,0:T(8,128)} %bitcast.20, f32[20,7,8,8,128]{4,3,2,1,0:T(8,128)} %bitcast.17, f32[7,7]{1,0:T(8,128)} %mixing.1, ...), custom_call_target="tpu_custom_call" | custom-call | tf_op jit(solution)/shard_map/krylov_block/pallas_call | solution.py:674
  40.2 4.9 %normalize.1 = (f32[4,7,8,8,128]{4,3,2,1,0:T(8,128)}, f32[4,20]{1,0:T(4,128)}, f32[4,4]{1,0:T(4,128)}) custom-call(f32[4,128]{1,0:T(4,128)} %get-tuple-element.8.packed_ref, s32[4,128]{1,0:T(4,128)} %constant.5.clone.pairs, f32[4,7,8,8,128]{4,3,2,1,0:T(8,128)} %get-tuple-element.9.krylov, f32[20,7,8,8,128]{4,3,2,1,0:T(8,128)} %bitcast.18), custom_call_target="tpu_custom_call" | custom-call | tf_op jit(solution)/shard_map/normalize/pallas_call | solution.py:716
